TPU v7x, 32 devices: a whole 2x2x4 slice. The times are simulated.
32 devices in a mesh: ctx: 8 (over z, x), tab: 4 (over y, core).
Axes of the slice: x: 2, y: 2, z: 4, core: 2. Of those that a mesh axis runs over, the one named last changes fastest.
Arguments:
- table: bfloat16 [8, 4, 4096, 512], P('ctx', 'tab'), may hold values from -6 to 6
- row_ids: int32 [8, 4, 256], P('ctx', 'tab'), may hold values from 0 to 4095
- dests: int32 [8, 4, 4], P('ctx'), may hold values from 0 to 3, as said below
- slots: int32 [8, 4, 4], P('ctx'), may hold values from 0 to 3, as said below
- lengths: int32 [4, 16], P('tab'), may hold values from 1 to 1024, 2048 in all within a row
- tile_mask: int32 [4, 32, 32], P('tab'), may hold values from 0 to 1, as said below
- w_in: bfloat16 [512, 2048], replicated, may hold values from -0.25 to 0.25
- w_out: bfloat16 [512, 512], replicated, may hold values from -0.25 to 0.25
- output_gradient: bfloat16 [4, 2048, 512], P('tab', 'ctx'), may hold values from -6 to 6
Outputs:
- layer_out: bfloat16 [4, 2048, 512], P('tab', 'ctx')
- table_grad: bfloat16 [8, 4, 4096, 512], P('ctx', 'tab')
Inputs may be any that keep to these rules, and one draw needn't show every extreme that they name: `dests`: the 4 blocks of one device go to 4 different indices of tab, and every device of a ctx index receives exactly one block for each slot 0 to 3. `slots`: see dests. `lengths`: each row sums to 2048; its longest history has exactly 1024 positions. `tile_mask`: diagonal tiles are 1.
All inputs are finite; a program needn't handle non-finite values.
Results may differ from a plain program's by a relative error of at most 0.012.
Values may be sent and summed in bfloat16 or wider, within the bound.
A program may use at most 192 MiB of HBM per device.

v0:
```python
import jax
import jax.numpy as jnp
from jax import lax
from jax.sharding import PartitionSpec as P

H = 4
BROWS = 64
NBLK = 4


epsilon = 1e-05


def layer_statistics(inputs):
    row_mean = jnp.mean(inputs, axis=-1, keepdims=True)
    centred = inputs - row_mean
    inverse = lax.rsqrt(jnp.mean(centred * centred, axis=-1, keepdims=True) + epsilon)
    return (centred * inverse, inverse)


def norm_backward_pass(incoming_gradient, normalized_rows, inverse):
    first = jnp.mean(incoming_gradient, axis=-1, keepdims=True)
    second = jnp.mean(incoming_gradient * normalized_rows, axis=-1, keepdims=True)
    return inverse * (incoming_gradient - first - normalized_rows * second)


def silu_slope(argument):
    sigmoid_v = jax.nn.sigmoid(argument)
    return sigmoid_v * (1.0 + argument * (1.0 - sigmoid_v))


def position_of(stored, rows_dev, chain_count):
    half = rows_dev // 2
    owner = stored // rows_dev
    local = stored % rows_dev
    early = owner * half + local
    late = (2 * chain_count - 1 - owner) * half + local - half
    return jnp.where(local < half, early, late)


def doc_index(position, doc_ends):
    return jnp.sum((position[:, None] >= doc_ends[None, :]).astype(jnp.int32), axis=1)


def pair_mask(query_pos, key_pos, doc_ends, tile_table):
    same_doc = doc_index(query_pos, doc_ends)[:, None] == doc_index(key_pos, doc_ends)[None, :]
    causal = key_pos[None, :] <= query_pos[:, None]
    tile_ids = jnp.arange(tile_table.shape[0], dtype=jnp.int32)
    query_pick = ((query_pos // BROWS)[:, None] == tile_ids[None, :]).astype(jnp.float32)
    key_pick = ((key_pos // BROWS)[None, :] == tile_ids[:, None]).astype(jnp.float32)
    picked = jnp.dot(query_pick, tile_table, precision=lax.Precision.HIGHEST)
    tile_on = jnp.dot(picked, key_pick, precision=lax.Precision.HIGHEST) > 0.5
    return (same_doc & causal & tile_on).astype(jnp.float32)


def pair_terms(query_heads, grad_heads, key_heads, value_heads, allowed, score_scale):
    scores = (
        jnp.einsum("qhd,khd->hqk", query_heads, key_heads, preferred_element_type=jnp.float32)
        * score_scale
    )
    probs = (jax.nn.silu(scores) * allowed[None]).astype(jnp.bfloat16)
    d_probs = jnp.einsum(
        "qhd,khd->hqk", grad_heads, value_heads, preferred_element_type=jnp.float32
    )
    d_scores = (d_probs * silu_slope(scores) * allowed[None] * score_scale).astype(jnp.bfloat16)
    return (probs, d_scores)


def body(table, row_ids, dests, slots, lengths, tile_mask, w_in, w_out, output_gradient):
    tab_count = lax.axis_size("tab")
    ctx_count = lax.axis_size("ctx")
    own_tab = lax.axis_index("tab")
    own_ctx = lax.axis_index("ctx")
    row_count = row_ids.shape[2]
    model_width = w_out.shape[0]
    head_dim = model_width // H
    score_scale = head_dim ** (-0.5)
    own_pos = position_of(
        own_ctx * row_count + jnp.arange(row_count, dtype=jnp.int32), row_count, ctx_count
    )
    doc_ends = jnp.cumsum(lengths[0])
    tile_table = tile_mask[0].astype(jnp.float32)
    looked_rows = jnp.take(table[0, 0], row_ids[0, 0], axis=0).reshape(NBLK, BROWS, model_width)
    route_dest = dests[0]
    route_slot = slots[0]
    own_dest = lax.dynamic_index_in_dim(route_dest, own_tab, 0, keepdims=False)
    tab_ids = jnp.arange(tab_count, dtype=jnp.int32)
    send_pick = (own_dest[None, :] == tab_ids[:, None]).astype(jnp.bfloat16)
    outgoing = jnp.einsum(
        "tp,prd->trd", send_pick, looked_rows, preferred_element_type=jnp.float32
    ).astype(jnp.bfloat16)
    arrived = lax.all_to_all(outgoing, "tab", split_axis=0, concat_axis=0, tiled=True)
    slot_ids = jnp.arange(NBLK, dtype=jnp.int32)
    slot_hits = (route_dest == own_tab)[None, :, :] & (
        route_slot[None, :, :] == slot_ids[:, None, None]
    )
    receive_pick = jnp.sum(slot_hits.astype(jnp.int32), axis=2).astype(jnp.bfloat16)
    user_sequence = jnp.einsum(
        "st,trd->srd", receive_pick, arrived, preferred_element_type=jnp.float32
    )
    user_sequence = user_sequence.astype(jnp.bfloat16).reshape(row_count, model_width)
    centred_scaled_input, inverse_deviation = layer_statistics(user_sequence.astype(jnp.float32))
    normalized_rows = centred_scaled_input.astype(jnp.bfloat16)
    pre = jnp.dot(normalized_rows, w_in, preferred_element_type=jnp.float32)
    act = jax.nn.silu(pre).astype(jnp.bfloat16)
    up_part = act[:, 0:model_width]
    value_part = act[:, model_width : 2 * model_width]
    query_part = act[:, 2 * model_width : 3 * model_width]
    key_part = act[:, 3 * model_width : 4 * model_width]
    query_heads = query_part.reshape(row_count, H, head_dim)
    zero_rows = jnp.zeros((row_count, model_width), jnp.float32)
    key_in = lax.all_gather(key_part, "ctx", axis=0, tiled=True)
    value_in = lax.all_gather(value_part, "ctx", axis=0, tiled=True)
    part_rows = key_in.shape[0]
    key_pos = position_of(jnp.arange(part_rows, dtype=jnp.int32), row_count, ctx_count)
    allowed = pair_mask(own_pos, key_pos, doc_ends, tile_table)

    def attend_compute(total):
        scores = (
            jnp.einsum(
                "qhd,khd->hqk",
                query_heads,
                key_in.reshape(part_rows, H, head_dim),
                preferred_element_type=jnp.float32,
            )
            * score_scale
        )
        probs = (jax.nn.silu(scores) * allowed[None]).astype(jnp.bfloat16)
        update = jnp.einsum(
            "hqk,khd->qhd",
            probs,
            value_in.reshape(part_rows, H, head_dim),
            preferred_element_type=jnp.float32,
        )
        return update.reshape(row_count, model_width)

    attn = lax.cond(jnp.any(allowed > 0.5), attend_compute, lambda total: total, zero_rows)
    attn_hat, attn_inverse = layer_statistics(attn)
    up_float = up_part.astype(jnp.float32)
    mixed = (attn_hat * up_float).astype(jnp.bfloat16)
    layer_out = (
        user_sequence.astype(jnp.float32)
        + jnp.dot(mixed, w_out, preferred_element_type=jnp.float32)
    ).astype(jnp.bfloat16)
    incoming_gradient = output_gradient[0]
    dmixed = jnp.dot(incoming_gradient, w_out.T, preferred_element_type=jnp.float32)
    d_up = dmixed * attn_hat
    d_attn = norm_backward_pass(dmixed * up_float, attn_hat, attn_inverse).astype(jnp.bfloat16)
    grad_heads = d_attn.reshape(row_count, H, head_dim)
    query_key_in = lax.all_gather(key_part, "ctx", axis=0, tiled=True)
    query_value_in = lax.all_gather(value_part, "ctx", axis=0, tiled=True)
    query_part_rows = query_key_in.shape[0]
    key_pos = position_of(jnp.arange(query_part_rows, dtype=jnp.int32), row_count, ctx_count)
    query_allowed = pair_mask(own_pos, key_pos, doc_ends, tile_table)

    def query_compute(total):
        key_heads = query_key_in.reshape(query_part_rows, H, head_dim)
        probs, d_scores = pair_terms(
            query_heads,
            grad_heads,
            key_heads,
            query_value_in.reshape(query_part_rows, H, head_dim),
            query_allowed,
            score_scale,
        )
        update = jnp.einsum("hqk,khd->qhd", d_scores, key_heads, preferred_element_type=jnp.float32)
        return update.reshape(row_count, model_width)

    d_query = lax.cond(jnp.any(query_allowed > 0.5), query_compute, lambda total: total, zero_rows)
    own_key_heads = key_part.reshape(row_count, H, head_dim)
    own_value_heads = value_part.reshape(row_count, H, head_dim)
    query_in = lax.all_gather(query_part, "ctx", axis=0, tiled=True)
    grad_in = lax.all_gather(d_attn, "ctx", axis=0, tiled=True)
    key_part_rows = query_in.shape[0]
    query_pos = position_of(jnp.arange(key_part_rows, dtype=jnp.int32), row_count, ctx_count)
    key_allowed = pair_mask(query_pos, own_pos, doc_ends, tile_table)

    def key_compute(totals):
        query_rows = query_in.reshape(key_part_rows, H, head_dim)
        grad_rows = grad_in.reshape(key_part_rows, H, head_dim)
        probs, d_scores = pair_terms(
            query_rows, grad_rows, own_key_heads, own_value_heads, key_allowed, score_scale
        )
        key_term = jnp.einsum(
            "hqk,qhd->khd", d_scores, query_rows, preferred_element_type=jnp.float32
        )
        value_term = jnp.einsum(
            "hqk,qhd->khd", probs, grad_rows, preferred_element_type=jnp.float32
        )
        return (
            key_term.reshape(row_count, model_width),
            value_term.reshape(row_count, model_width),
        )

    d_key, d_value = lax.cond(
        jnp.any(key_allowed > 0.5), key_compute, lambda totals: totals, (zero_rows, zero_rows)
    )
    d_act = jnp.concatenate([d_up, d_value, d_query, d_key], axis=1)
    d_pre = (d_act * silu_slope(pre)).astype(jnp.bfloat16)
    normalized_gradient = jnp.dot(d_pre, w_in.T, preferred_element_type=jnp.float32)
    sequence_gradient = (
        incoming_gradient.astype(jnp.float32)
        + norm_backward_pass(normalized_gradient, centred_scaled_input, inverse_deviation)
    ).astype(jnp.bfloat16)
    grad_blocks = sequence_gradient.reshape(NBLK, BROWS, model_width)
    returning = jnp.einsum(
        "st,srd->trd", receive_pick, grad_blocks, preferred_element_type=jnp.float32
    ).astype(jnp.bfloat16)
    came_back = lax.all_to_all(returning, "tab", split_axis=0, concat_axis=0, tiled=True)
    row_grads = jnp.einsum(
        "tp,trd->prd", send_pick, came_back, preferred_element_type=jnp.float32
    ).reshape(row_count, model_width)
    table_grad = (
        jnp.zeros((table.shape[2], model_width), jnp.float32)
        .at[row_ids[0, 0]]
        .add(row_grads)
        .astype(jnp.bfloat16)
    )
    return (
        layer_out.reshape(1, row_count, model_width),
        table_grad.reshape(1, 1, table.shape[2], model_width),
    )


def solution(mesh):
    in_specs = (
        P("ctx", "tab", None, None),
        P("ctx", "tab", None),
        P("ctx", None, None),
        P("ctx", None, None),
        P("tab", None),
        P("tab", None, None),
        P(),
        P(),
        P("tab", "ctx", None),
    )
    out_specs = (P("tab", "ctx", None), P("ctx", "tab", None, None))
    return jax.shard_map(body, mesh=mesh, in_specs=in_specs, out_specs=out_specs, check_vma=False)
```

profile of v0, /device:TPU:1, one launch (start us, length us, event | category | flops | bytes accessed | tf_op | source)
XLA Modules:
  0.0 301.4 jit_solution(6601176184997076878)
XLA Ops:
  7.2 0.8 compare_select_fusion
  8.0 0.5 broadcast.824
  8.5 1.3 reduce.8
  10.1 0.7 dynamic-slice_bitcast_fusion
  10.8 4.0 %gather_fusion = bf16[256,512]{1,0:T(8,128)(2,1)S(1)} fusion(bf16[4096,512]{1,0:T(8,128)(2,1)} %bitcast.132, s32[1024]{0:T(1024)S(1)} %pad_clamp_fusion), kind=kCustom, calls=%fused_computation | custom fusion | bytes 525312 | tf_op jit(solution)/shard_map/jit(_take)/gather | solution.py:83
  14.7 0.5 convolution_convert_fusion.2
  15.2 0.7 copy.119
  16.0 4.3 %all-to-all-start = ((bf16[4,64,512]{2,1,0:T(8,128)(2,1)}), bf16[4,64,512]{2,1,0:T(8,128)(2,1)S(1)}, u32[]{:S(2)}, u32[]{:S(2)}) async-start(bf16[4,64,512]{2,1,0:T(8,128)(2,1)} %copy.119), calls=%async_computation | async-start | bytes 524288 | tf_op jit(solution)/shard_map/all_to_all | solution.py:92
  20.4 4.9 %all-to-all-done = bf16[4,64,512]{2,1,0:T(8,128)(2,1)S(1)} async-done(((bf16[4,64,512]{2,1,0:T(8,128)(2,1)}), bf16[4,64,512]{2,1,0:T(8,128)(2,1)S(1)}, u32[]{:S(2)}, u32[]{:S(2)}) %all-to-all-start) | async-done | bytes 262176 | tf_op jit(solution)/shard_map/all_to_all | solution.py:92
  26.7 2.1 multiply_convert_fusion.5
  28.8 1.0 copy-done.2
  29.8 0.9 fusion.107
  30.8 0.7 all-gather.7.cloned.1.call-update
  31.5 0.7 all-gather.11.cloned.1.call-update
  33.0 3.4 %compare_reduce_fusion.1 = (pred[]{:T(512)}, f32[256,2048]{1,0:T(8,128)}) fusion(f32[256,32]{0,1:T(8,128)S(1)} %fusion.64, s32[2048]{0:T(1024)S(1)} %get-tuple-element.157, s32[256]{0:T(256)S(1)} %get-tuple-element.156, s32[2048]{0:T(1024)S(1)} %get-tuple-element.158, s32[2048]{0:T(1024)S(1)} %convert_reduce_fusion, s32[256]{0:T(256)S(1)} %convert_reduce_fusion.1), kind=kOutput, calls=%fused_computation.47 | convolution fusion | flops 205586432 | bytes 2156545 | tf_op jit(solution)/shard_map/dot_general | solution.py:52
  37.1 0.8 reshape.401
  37.9 42.4 %all-gather.5.cloned.1.call-done = bf16[2048,512]{1,0:T(8,128)(2,1)} async-done(((bf16[256,512]{1,0:T(8,128)(2,1)}), bf16[2048,512]{1,0:T(8,128)(2,1)}) %all-gather.5.cloned.1.call-update) | async-done | bytes 2097168 | tf_op jit(solution)/shard_map/all_gather | solution.py:112
  80.2 50.5 %all-gather.7.cloned.1.call-done = bf16[2048,512]{1,0:T(8,128)(2,1)} async-done(((bf16[256,512]{1,0:T(8,128)(2,1)}), bf16[2048,512]{1,0:T(8,128)(2,1)}) %all-gather.7.cloned.1.call-update) | async-done | bytes 2097168 | tf_op jit(solution)/shard_map/all_gather | solution.py:113
  130.8 13.5 %conditional.3 = (f32[256,1]{0,1:T(1,128)S(1)}, f32[256,512]{1,0:T(8,128)S(1)}) conditional(s32[]{:T(128)} %convert_element_type.116, () %tuple.32, (bf16[2048,512]{1,0:T(8,128)(2,1)}, bf16[256,4,128]{2,1,0:T(4,128)(2,1)}, f32[256,2048]{1,0:T(8,128)}, bf16[2048,512]{1,0:T(8,128)(2,1)}) %tuple.33), branch_computations={%region_7.8_spmd, %region_8.10_spmd} | conditional | flops 1088552704 | bytes 13370412 | solution.py:137
  130.8 4.0 %copy.127 = bf16[2048,512]{0,1:T(8,128)(2,1)} copy(bf16[2048,512]{1,0:T(8,128)(2,1)} %get-tuple-element.119) | data formatting | bytes 4194304 | tf_op jit(solution)/shard_map
  134.8 8.1 %fusion.102 = (f32[256]{0:T(256)S(1)}, f32[4,256,128]{1,2,0:T(8,128)}) fusion(bf16[2048,4,128]{0,2,1:T(8,128)(2,1)} %bitcast.130, f32[256,2048]{1,0:T(8,128)} %get-tuple-element.38, bf16[256,4,128]{2,1,0:T(4,128)(2,1)S(1)} %copy-done.7, bf16[2048,512]{1,0:T(8,128)(2,1)} %get-tuple-element.37), kind=kOutput, calls=%fused_computation.164 | convolution fusion | flops 1088552704 | bytes 7078912 | tf_op jit(solution)/shard_map/cond/branch_1_fun/hqk,khd->qhd/dot_general | solution.py:129
  142.8 1.2 copy.149
  144.5 1.6 fusion.61
  146.1 2.1 fusion.49
  148.2 0.8 fusion.42
  149.1 3.4 %compare_reduce_fusion = (pred[]{:T(512)}, f32[2048,256]{1,0:T(8,128)}) fusion(f32[2048,32]{0,1:T(8,128)S(1)} %fusion.42, s32[256]{0:T(256)S(1)} %get-tuple-element.155, s32[2048]{0:T(1024)S(1)} %get-tuple-element.158, s32[256]{0:T(256)S(1)} %get-tuple-element.156, s32[256]{0:T(256)S(1)} %convert_reduce_fusion.1, s32[2048]{0:T(1024)S(1)} %convert_reduce_fusion), kind=kOutput, calls=%fused_computation.46 | convolution fusion | flops 205529088 | bytes 2378753 | tf_op jit(solution)/shard_map/dot_general | solution.py:52
  153.1 23.3 %conditional.5 = (f32[256,512]{1,0:T(8,128)}) conditional(s32[]{:T(128)} %convert_element_type.116, () %tuple.36, (bf16[256,512]{1,0:T(8,128)(2,1)}, bf16[2048,512]{1,0:T(8,128)(2,1)}, bf16[2048,512]{1,0:T(8,128)(2,1)}, bf16[256,4,128]{2,1,0:T(4,128)(2,1)}, f32[256,2048]{1,0:T(8,128)}) %tuple.37), branch_computations={%region_16.17_spmd, %region_17.18_spmd} | conditional | flops 1635778560 | bytes 29360136 | solution.py:169
  153.1 6.2 %fusion.22 = f32[4,256,2048]{2,1,0:T(8,128)} fusion(bf16[2048,512]{1,0:T(8,128)(2,1)} %get-tuple-element.46, bf16[256,512]{1,0:T(8,128)(2,1)} %get-tuple-element.45), kind=kOutput, calls=%fused_computation.24 | convolution fusion | flops 536870912 | bytes 10747904 | tf_op jit(solution)/shard_map/cond/branch_1_fun/qhd,khd->hqk/dot_general | solution.py:62
  159.3 4.1 %copy.131 = bf16[2048,512]{0,1:T(8,128)(2,1)} copy(bf16[2048,512]{1,0:T(8,128)(2,1)} %get-tuple-element.127) | data formatting | bytes 4194304 | tf_op jit(solution)/shard_map
  163.4 11.0 %fusion.25 = f32[4,256,128]{1,2,0:T(8,128)} fusion(bf16[2048,4,128]{0,2,1:T(8,128)(2,1)} %bitcast.131, f32[4,256,2048]{2,1,0:T(8,128)} %fusion.22, f32[256,2048]{1,0:T(8,128)} %get-tuple-element.49, bf16[256,4,128]{2,1,0:T(4,128)(2,1)} %get-tuple-element.128), kind=kOutput, calls=%fused_computation.27 | convolution fusion | flops 1098907648 | bytes 13369344 | tf_op jit(solution)/shard_map/cond/branch_1_fun/hqk,khd->qhd/dot_general | solution.py:166
  174.3 2.0 copy.155
  176.4 4.5 %all-gather.11.cloned.1.call-done = bf16[2048,512]{1,0:T(8,128)(2,1)} async-done(((bf16[256,512]{1,0:T(8,128)(2,1)}), bf16[2048,512]{1,0:T(8,128)(2,1)}) %all-gather.11.cloned.1.call-update) | async-done | bytes 2097168 | tf_op jit(solution)/shard_map/all_gather | solution.py:172
  180.9 49.8 %all-gather.9.cloned.1.call-done = bf16[2048,512]{1,0:T(8,128)(2,1)} async-done(((bf16[256,512]{1,0:T(8,128)(2,1)}), bf16[2048,512]{1,0:T(8,128)(2,1)}) %all-gather.9.cloned.1.call-update) | async-done | bytes 2097168 | tf_op jit(solution)/shard_map/all_gather | solution.py:173
  230.6 36.9 %conditional.4 = (f32[256,512]{1,0:T(8,128)}, f32[256,512]{1,0:T(8,128)}) conditional(s32[]{:T(128)} %convert_element_type.125, () %tuple.34, (bf16[2048,512]{1,0:T(8,128)(2,1)}, bf16[256,512]{1,0:T(8,128)(2,1)}, bf16[2048,512]{1,0:T(8,128)(2,1)}, bf16[256,512]{1,0:T(8,128)(2,1)S(1)}, f32[2048,256]{1,0:T(8,128)}) %tuple.90), branch_computations={%region_14.15_spmd, %region_15.16_spmd} | conditional | flops 2187329536 | bytes 50855980 | solution.py:195
  230.6 4.0 %copy.130 = bf16[2048,512]{0,1:T(8,128)(2,1)} copy(bf16[2048,512]{1,0:T(8,128)(2,1)} %get-tuple-element.122) | data formatting | bytes 4194304 | tf_op jit(solution)/shard_map
  234.6 6.1 %fusion.15 = f32[4,2048,256]{2,1,0:T(8,128)} fusion(bf16[2048,4,128]{0,2,1:T(8,128)(2,1)} %bitcast.126, bf16[256,512]{1,0:T(8,128)(2,1)S(1)} %get-tuple-element.43), kind=kOutput, calls=%fused_computation.16 | convolution fusion | flops 536870912 | bytes 10747904 | tf_op jit(solution)/shard_map/cond/branch_1_fun/qhd,khd->hqk/dot_general | solution.py:58
  240.7 4.0 %copy.129 = bf16[2048,512]{0,1:T(8,128)(2,1)} copy(bf16[2048,512]{1,0:T(8,128)(2,1)} %get-tuple-element.120) | data formatting | bytes 4194304 | tf_op jit(solution)/shard_map
  244.7 10.7 %fusion.10 = f32[4,256,128]{1,2,0:T(8,128)} fusion(bf16[2048,4,128]{0,2,1:T(8,128)(2,1)} %bitcast.127, f32[4,2048,256]{2,1,0:T(8,128)} %fusion.15, bf16[2048,4,128]{0,2,1:T(8,128)(2,1)} %bitcast.128, f32[2048,256]{1,0:T(8,128)} %get-tuple-element.44, bf16[256,512]{1,0:T(8,128)(2,1)S(1)} %copy-done.4), kind=kOutput, calls=%fused_computation.13 | convolution fusion | flops 1098907648 | bytes 15466496 | tf_op jit(solution)/shard_map/cond/branch_1_fun/hqk,qhd->khd/dot_general | solution.py:184
  255.4 2.1 copy.153
  257.5 8.1 %fusion.9 = f32[4,256,128]{1,2,0:T(8,128)} fusion(bf16[2048,4,128]{0,2,1:T(8,128)(2,1)} %bitcast.129, f32[4,2048,256]{2,1,0:T(8,128)} %fusion.15, f32[2048,256]{1,0:T(8,128)} %get-tuple-element.44), kind=kOutput, calls=%fused_computation.12 | convolution fusion | flops 551550976 | bytes 13107200 | tf_op jit(solution)/shard_map/cond/branch_1_fun/hqk,qhd->khd/dot_general | solution.py:187
  265.5 2.0 copy.151
  267.6 3.4 %fusion.101 = (f32[256]{0:T(256)S(1)}, f32[256]{0:T(256)S(1)}, f32[256,512]{1,0:T(8,128)S(1)}) fusion(f32[256]{0:T(256)S(1)} %rsqrt.20, f32[256]{0:T(256)S(1)} %div.124, f32[4,64,512]{2,1,0:T(8,128)S(1)} %copy.121, bf16[512,2048]{1,0:T(8,128)(2,1)S(1)} %copy-done, f32[256,512]{1,0:T(8,128)} %get-tuple-element.132, f32[256,512]{1,0:T(8,128)} %get-tuple-element.133, ...), kind=kOutput, calls=%fused_computation.163 | convolution fusion | flops 543817216 | bytes 7344128 | tf_op jit(solution)/shard_map/dot_general | solution.py:200
  271.6 0.7 copy.138
  272.3 5.2 %all-to-all-start.1 = ((bf16[4,64,512]{2,1,0:T(8,128)(2,1)}), bf16[4,64,512]{2,1,0:T(8,128)(2,1)S(1)}, u32[]{:S(2)}, u32[]{:S(2)}) async-start(bf16[4,64,512]{2,1,0:T(8,128)(2,1)} %copy.138), calls=%async_computation.1 | async-start | bytes 524288 | tf_op jit(solution)/shard_map/all_to_all | solution.py:209
  277.5 2.2 fusion.41
  279.7 3.0 all-to-all-done.1
  283.2 5.8 %scatter_custom_fusion = f32[4096,512]{1,0:T(8,128)} fusion(s32[256]{0:T(256)S(1)} %bitcast.145, f32[256,512]{1,0:T(8,128)S(1)} %bitcast.134, f32[]{:T(128)} %constant.184.clone.1), kind=kCustom, calls=%fused_computation.34 | custom fusion | flops 131072 | bytes 8388612 | tf_op jit(solution)/shard_map/scatter-add | solution.py:216
  289.0 5.9 %convert_bitcast_fusion = bf16[1,1,4096,512]{3,2,1,0:T(8,128)(2,1)} fusion(f32[4096,512]{1,0:T(8,128)} %scatter_custom_fusion), kind=kLoop, calls=%fused_computation.33 | loop fusion | flops 2097152 | bytes 12582912 | tf_op jit(solution)/shard_map/reshape | solution.py:221
  (64 shorter events, 3.9 us)
Async XLA Ops:
  7.2 19.5 %copy-start = (bf16[512,2048]{1,0:T(8,128)(2,1)S(1)}, bf16[512,2048]{1,0:T(8,128)(2,1)}, u32[]{:S(2)}) copy-start(bf16[512,2048]{1,0:T(8,128)(2,1)} %param.21) | copy-start | bytes 6291460
  10.8 9.5 %copy-start.9 = (s32[1,4,4]{2,1,0:T(4,128)S(1)}, s32[1,4,4]{2,1,0:T(4,128)}, u32[]{:S(2)}) copy-start(s32[1,4,4]{2,1,0:T(4,128)} %param.17) | copy-start | bytes 196
  10.8 9.5 %copy-start.10 = (s32[1,4,4]{2,1,0:T(4,128)S(1)}, s32[1,4,4]{2,1,0:T(4,128)}, u32[]{:S(2)}) copy-start(s32[1,4,4]{2,1,0:T(4,128)} %param.18) | copy-start | bytes 196
  16.0 9.3 %all-to-all-start = ((bf16[4,64,512]{2,1,0:T(8,128)(2,1)}), bf16[4,64,512]{2,1,0:T(8,128)(2,1)S(1)}, u32[]{:S(2)}, u32[]{:S(2)}) async-start(bf16[4,64,512]{2,1,0:T(8,128)(2,1)} %copy.119), calls=%async_computation | async-start | bytes 524288 | tf_op jit(solution)/shard_map/all_to_all | solution.py:92
  20.3 60.0 %all-gather.5.cloned.1.call-start = ((), (), s32[]{:S(2)}) async-start(), calls=%async_computation.2 | async-start | bytes 2359296 | tf_op jit(solution)/shard_map/all_gather | solution.py:112
  28.8 1.0 copy-start.2
  28.8 3.5 %copy-start.11 = (s32[1,16]{1,0:T(1,128)S(1)}, s32[1,16]{1,0:T(1,128)}, u32[]{:S(2)}) copy-start(s32[1,16]{1,0:T(1,128)} %param.19) | copy-start | bytes 196
  28.8 3.9 %copy-start.8 = (s32[1,32,32]{2,1,0:T(8,128)S(1)}, s32[1,32,32]{2,1,0:T(8,128)}, u32[]{:S(2)}) copy-start(s32[1,32,32]{2,1,0:T(8,128)} %param.20) | copy-start | bytes 12292
  30.7 100.0 %all-gather.7.cloned.1.call-start = ((), (), s32[]{:S(2)}) async-start(), calls=%async_computation.3 | async-start | bytes 2359296 | tf_op jit(solution)/shard_map/all_gather | solution.py:113
  30.8 6.3 %copy-start.1 = (bf16[256,512]{1,0:T(8,128)(2,1)S(1)}, bf16[256,512]{1,0:T(8,128)(2,1)}, u32[]{:S(2)}) copy-start(bf16[256,512]{1,0:T(8,128)(2,1)} %get-tuple-element.143) | copy-start | bytes 786436
  31.5 149.4 %all-gather.11.cloned.1.call-start = ((), (), s32[]{:S(2)}) async-start(), calls=%async_computation.5 | async-start | bytes 2359296 | tf_op jit(solution)/shard_map/all_gather | solution.py:172
  32.2 198.4 %all-gather.9.cloned.1.call-start = ((), (), s32[]{:S(2)}) async-start(), calls=%async_computation.4 | async-start | bytes 2359296 | tf_op jit(solution)/shard_map/all_gather | solution.py:173
  130.8 13.7 %copy-start.5 = (bf16[1,256,512]{2,1,0:T(8,128)(2,1)S(1)}, bf16[1,256,512]{2,1,0:T(8,128)(2,1)}, u32[]{:S(2)}) copy-start(bf16[1,256,512]{2,1,0:T(8,128)(2,1)} %param.23) | copy-start | bytes 786436
  130.8 4.0 %copy-start.7 = (bf16[256,4,128]{2,1,0:T(4,128)(2,1)S(1)}, bf16[256,4,128]{2,1,0:T(4,128)(2,1)}, u32[]{:S(2)}) copy-start(bf16[256,4,128]{2,1,0:T(4,128)(2,1)} %get-tuple-element.117) | copy-start | bytes 786436 | tf_op jit(solution)/shard_map/cond
  153.0 77.6 %copy-start.3 = (bf16[256,512]{1,0:T(8,128)(2,1)S(1)}, bf16[256,512]{1,0:T(8,128)(2,1)}, u32[]{:S(2)}) copy-start(bf16[256,512]{1,0:T(8,128)(2,1)} %get-tuple-element.144) | copy-start | bytes 786436
  240.7 4.0 %copy-start.4 = (bf16[256,512]{1,0:T(8,128)(2,1)S(1)}, bf16[256,512]{1,0:T(8,128)(2,1)}, u32[]{:S(2)}) copy-start(bf16[256,512]{1,0:T(8,128)(2,1)} %get-tuple-element.41) | copy-start | bytes 786436 | tf_op jit(solution)/shard_map/cond
  267.6 3.4 %copy-start.6 = (bf16[1,256,512]{2,1,0:T(8,128)(2,1)S(1)}, bf16[1,256,512]{2,1,0:T(8,128)(2,1)}, u32[]{:S(2)}) copy-start(bf16[1,256,512]{2,1,0:T(8,128)(2,1)} %param.23) | copy-start | bytes 786436
  272.3 10.3 %all-to-all-start.1 = ((bf16[4,64,512]{2,1,0:T(8,128)(2,1)}), bf16[4,64,512]{2,1,0:T(8,128)(2,1)S(1)}, u32[]{:S(2)}, u32[]{:S(2)}) async-start(bf16[4,64,512]{2,1,0:T(8,128)(2,1)} %copy.138), calls=%async_computation.1 | async-start | bytes 524288 | tf_op jit(solution)/shard_map/all_to_all | solution.py:209
Sparse Core Ops, SparseCore 0:
  30.8 49.3 all-gather.4
  82.9 47.7 all-gather.6
  132.9 47.9 all-gather.10
  182.8 47.7 all-gather.8
where the time goes:
time: 303 us; the launch traced here: 301 us
  waiting for transfers between devices  156 us (51%)
  matrix products  68.8 us (23%)
  local copies, waits for them, and re-layouts  33.7 us (11%)
  other arithmetic  17.4 us (6%)
  between operations  15.3 us (5%)
  starting transfers between devices  9.57 us (3%)
    all_gather x1, waiting for transfers between devices, body(): value_in = lax.all_gather(value_part, 'ctx', axis=0, tiled=True)  50.5 us
    all_gather x1, waiting for transfers between devices, body(): grad_in = lax.all_gather(d_attn, 'ctx', axis=0, tiled=True)  49.8 us
    all_gather x1, waiting for transfers between devices, body(): key_in = lax.all_gather(key_part, 'ctx', axis=0, tiled=True)  42.4 us
    another operation x5, local copies, waits for them, and re-layouts  16.1 us
    dot_general x1, matrix products, query_compute(): jnp.einsum('hqk,khd->qhd', d_scores, key_heads, preferred_element_type=jn...  11 us
    dot_general x1, matrix products, key_compute(): jnp.einsum('hqk,qhd->khd', d_scores, query_rows, preferred_element_type=j...  10.7 us
    dot_general x1, matrix products, attend_compute(): jnp.einsum('hqk,khd->qhd', probs, value_in.reshape(part_rows, H, head_dim...  8.07 us
    dot_general x1, matrix products, key_compute(): jnp.einsum('hqk,qhd->khd', probs, grad_rows, preferred_element_type=jnp.f...  8.06 us
  transfers between devices with their start and end apart: 6, of which 6 were waited for; matrix products, arithmetic and copies ran while one was open for 17% of the time, Pallas kernels for 0%

commit v1 on v0

v1 whole, which is shorter than its diff:
```python
import functools

import jax
import jax.numpy as jnp
from jax import lax
from jax.experimental import pallas as pl
from jax.experimental.pallas import tpu as pltpu
from jax.sharding import PartitionSpec as P

H = 4
BROWS = 64
NBLK = 4
FAST = 2

epsilon = 1e-05
MESH = pl.DeviceIdType.MESH
NT = (((1,), (1,)), ((), ()))
TN = (((0,), (0,)), ((), ()))


def dot(a, b):
    return jnp.dot(a, b, preferred_element_type=jnp.float32)


def dot_nt(a, b):
    return lax.dot_general(a, b, NT, preferred_element_type=jnp.float32)


def layer_statistics(inputs):
    row_mean = jnp.mean(inputs, axis=-1, keepdims=True)
    centred = inputs - row_mean
    inverse = lax.rsqrt(jnp.mean(centred * centred, axis=-1, keepdims=True) + epsilon)
    return (centred * inverse, inverse)


def norm_backward_pass(incoming, normalized, inverse):
    first = jnp.mean(incoming, axis=-1, keepdims=True)
    second = jnp.mean(incoming * normalized, axis=-1, keepdims=True)
    return inverse * (incoming - first - normalized * second)


def silu_half(half):
    return half * (1.0 + jnp.tanh(half))


def slope_half(half, tanh):
    return (0.5 + 0.5 * tanh) * (1.0 + half * (1.0 - tanh))


def lookup_kernel(ids_ref, table_ref, out_ref, acc):
    step = pl.program_id(0)
    rows = table_ref.shape[2]
    count = ids_ref.shape[2]

    @pl.when(step == 0)
    def _():
        acc[...] = jnp.zeros_like(acc)

    base = step * rows
    row = lax.broadcasted_iota(jnp.int32, (rows, count), 0) + base
    pick = jnp.where(row == ids_ref[0], 1.0, 0.0).astype(jnp.bfloat16)
    acc[...] += lax.dot_general(
        pick, table_ref[0, 0], TN, preferred_element_type=jnp.float32
    )

    @pl.when(step == pl.num_programs(0) - 1)
    def _():
        out_ref[...] = acc[...].astype(out_ref.dtype)


def scatter_kernel(ids_ref, grads_ref, out_ref):
    rows = out_ref.shape[2]
    count = ids_ref.shape[2]
    row = lax.broadcasted_iota(jnp.int32, (rows, count), 0) + pl.program_id(0) * rows
    pick = jnp.where(row == ids_ref[0], 1.0, 0.0).astype(jnp.bfloat16)
    out_ref[0, 0] = dot(pick, grads_ref[...]).astype(out_ref.dtype)


def layer_kernel(
    n,
    tabs,
    dests,
    slots,
    lengths,
    tiles,
    rows_ref,
    w_in,
    w_out,
    og_ref,
    out_ref,
    grads_ref,
    xg,
    dg,
    vqk,
    gq,
    pk,
    gk,
    pre,
    attn,
    seq,
    dq,
    dk,
    dv,
    dup,
    startq,
    route_out,
    route_in,
    back_out,
    back_in,
    xs,
    xr,
    ds_,
    dr,
    rs,
    rr,
    bs,
    br,
):
    me = lax.axis_index("ctx")
    tab = lax.axis_index("tab")
    levels = n // FAST
    z = me // FAST
    x = me % FAST
    rows = rows_ref.shape[0]
    width = rows_ref.shape[1]
    half = rows // 2
    per_half = half // BROWS
    hd = width // H
    scale = hd ** (-0.5)

    barrier = pltpu.get_barrier_semaphore()

    def greet_ctx(k, carry):
        pl.semaphore_signal(
            barrier, inc=1, device_id=(lax.rem(me + k, n), tab), device_id_type=MESH
        )
        return carry

    def greet_tab(k, carry):
        pl.semaphore_signal(
            barrier, inc=1, device_id=(me, lax.rem(tab + k, tabs)), device_id_type=MESH
        )
        return carry

    lax.fori_loop(1, n, greet_ctx, 0)
    lax.fori_loop(1, tabs, greet_tab, 0)

    def choose(hit, block, other):
        on = jnp.full(block.shape, hit.astype(jnp.int32)) > 0
        return jnp.where(on, block, other)

    def block_for(t):
        block = rows_ref[0:BROWS, :]
        for p in range(1, NBLK):
            other = rows_ref[p * BROWS : (p + 1) * BROWS, :]
            block = choose(dests[0, tab, p] == t, other, block)
        return block

    def route_copy(src, dst, send, recv, t):
        return pltpu.make_async_remote_copy(
            src_ref=src.at[t],
            dst_ref=dst.at[tab],
            send_sem=send.at[t],
            recv_sem=recv.at[tab],
            device_id=(me, t),
            device_id_type=MESH,
        )

    def route_wait(src, dst, send, recv, t):
        pltpu.make_async_remote_copy(
            src_ref=src.at[t],
            dst_ref=dst.at[t],
            send_sem=send.at[t],
            recv_sem=recv.at[t],
            device_id=(me, t),
            device_id_type=MESH,
        ).wait()

    for k in range(tabs):
        t = lax.rem(tab + k, tabs)
        if k == 0:
            route_in[tab] = block_for(t)
        else:
            route_out[t] = block_for(t)

    pl.semaphore_wait(barrier, n + tabs - 2)

    for k in range(1, tabs):
        route_copy(route_out, route_in, rs, rr, lax.rem(tab + k, tabs)).start()

    def starts_of(pos):
        end = jnp.int32(0)
        start = jnp.zeros_like(pos)
        for e in range(lengths.shape[1]):
            end = end + lengths[0, e]
            start = jnp.where(pos >= end, end, start)
        return start

    def positions(s, shape, dim):
        local = lax.broadcasted_iota(jnp.int32, shape, dim)
        return local + jnp.where(local < half, s * half, (2 * n - 1 - s) * half - half)

    startq[...] = starts_of(positions(me, (rows, 128), 0))
    attn[...] = jnp.zeros_like(attn)

    def tile_id(s, a):
        if a < per_half:
            return s * per_half + a
        return (2 * n - 1 - s) * per_half + a - per_half

    count = 2 * per_half

    def tile_rows(pick):
        block = lax.broadcasted_iota(jnp.int32, (BROWS, rows), 1) // BROWS
        stripes = []
        for a in range(count):
            line = jnp.zeros((BROWS, rows), jnp.int32)
            for b in range(count):
                line = jnp.where(block == b, pick(a, b), line)
            stripes.append(line)
        return jnp.concatenate(stripes, axis=0) > 0

    def query_mask(s):
        own = positions(me, (rows, rows), 0)
        other = positions(s, (rows, rows), 1)
        first = jnp.broadcast_to(startq[:, 0:1], (rows, rows))
        on = tile_rows(lambda a, b: tiles[0, tile_id(me, a), tile_id(s, b)])
        return jnp.where((other <= own) & (other >= first) & on, 1.0, 0.0)

    def key_mask(s):
        own = positions(me, (rows, rows), 0)
        other = positions(s, (rows, rows), 1)
        first = starts_of(positions(s, (1, rows), 1))
        on = tile_rows(lambda a, b: tiles[0, tile_id(s, b), tile_id(me, a)])
        return jnp.where((own <= other) & (own >= first) & on, 1.0, 0.0)

    def take(buf, part, s, h):
        return buf[part, s, :, h * hd : (h + 1) * hd]

    def project(s):
        block = xg[s]
        for part in range(3):
            lo = (part + 1) * width
            value = dot(block, w_in[:, lo : lo + width])
            vqk[part, s] = silu_half(0.5 * value).astype(jnp.bfloat16)

    def forward(s):
        project(s)
        mask = query_mask(s)
        for h in range(H):
            cut = slice(h * hd, (h + 1) * hd)
            halfs = dot_nt(take(vqk, 1, me, h), take(vqk, 2, s, h)) * (0.5 * scale)
            tanh = jnp.tanh(halfs)
            probs = (halfs * (1.0 + tanh) * mask).astype(jnp.bfloat16)
            gq[s, h] = (slope_half(halfs, tanh) * (mask * scale)).astype(jnp.bfloat16)
            attn[:, cut] += dot(probs, take(vqk, 0, s, h))
        mask = key_mask(s)
        for h in range(H):
            halfs = dot_nt(take(vqk, 2, me, h), take(vqk, 1, s, h)) * (0.5 * scale)
            tanh = jnp.tanh(halfs)
            pk[s, h] = (halfs * (1.0 + tanh) * mask).astype(jnp.bfloat16)
            gk[s, h] = (slope_half(halfs, tanh) * (mask * scale)).astype(jnp.bfloat16)

    def query_back(s):
        for h in range(H):
            cut = slice(h * hd, (h + 1) * hd)
            slope = gq[s, h].astype(jnp.float32)
            dsc = dot_nt(dg[me, :, cut], take(vqk, 0, s, h)) * slope
            dq[:, cut] += dot(dsc.astype(jnp.bfloat16), take(vqk, 2, s, h))

    def key_back(s):
        for h in range(H):
            cut = slice(h * hd, (h + 1) * hd)
            grad = dg[s, :, cut]
            slope = gk[s, h].astype(jnp.float32)
            dsc = dot_nt(take(vqk, 0, me, h), grad) * slope
            dk[:, cut] += dot(dsc.astype(jnp.bfloat16), take(vqk, 1, s, h))
            dv[:, cut] += dot(pk[s, h], grad)

    def gather(buf, send, recv, compute, filler):
        def copy(s, way):
            to = (me - FAST, me + FAST, z * FAST + (FAST - 1 - x))[way]
            return pltpu.make_async_remote_copy(
                src_ref=buf.at[s],
                dst_ref=buf.at[s],
                send_sem=send.at[way, s],
                recv_sem=recv.at[s],
                device_id=(to, tab),
                device_id_type=MESH,
            )

        def ways(zz, action):
            s = zz * FAST + x

            @pl.when((zz >= z) & (z > 0))
            def _():
                action(copy(s, 0))

            @pl.when((zz <= z) & (z < levels - 1))
            def _():
                action(copy(s, 1))

            action(copy(s, 2))

        def level(j):
            far = (j + 1) // 2
            return z + jnp.where(j % 2 == 1, -far, far)

        def step(j, carry):
            zz = level(j)

            @pl.when((j < 2 * levels - 1) & (zz >= 0) & (zz < levels))
            def _():
                s = zz * FAST + x

                @pl.when(j > 0)
                def _():
                    copy(s, 2).wait_recv()

                ways(zz, lambda c: c.start())
                compute(s)

            if filler is not None:
                filler(j)
            before = level(j - 1)

            @pl.when((j > 0) & (before >= 0) & (before < levels))
            def _():
                s = before * FAST + (FAST - 1 - x)
                copy(s, 2).wait_recv()
                compute(s)

            return carry

        lax.fori_loop(0, 2 * levels, step, 0)

        def drain(zz, carry):
            ways(zz, lambda c: c.wait_send())
            return carry

        lax.fori_loop(0, levels, drain, 0)

    for k in range(1, tabs):
        route_wait(route_out, route_in, rs, rr, lax.rem(tab + k, tabs))

    def arrives(s, t):
        count = jnp.int32(0)
        for p in range(NBLK):
            hit = (dests[0, t, p] == tab) & (slots[0, t, p] == s)
            count += hit.astype(jnp.int32)
        return count > 0

    for s in range(NBLK):
        block = route_in[0]
        for t in range(1, tabs):
            block = choose(arrives(s, t), route_in[t], block)
        seq[s * BROWS : (s + 1) * BROWS, :] = block

    xhat, inverse = layer_statistics(seq[...].astype(jnp.float32))
    xg[me] = xhat.astype(jnp.bfloat16)

    gather(xg, xs, xr, forward, None)

    for part in range(4):
        pre[part] = 0.5 * dot(xg[me], w_in[:, part * width : (part + 1) * width])
    up = silu_half(pre[0]).astype(jnp.bfloat16).astype(jnp.float32)
    attn_hat, attn_inverse = layer_statistics(attn[...])
    dmixed = dot_nt(og_ref[0], w_out[...])
    dup[...] = dmixed * attn_hat
    dg[me] = norm_backward_pass(dmixed * up, attn_hat, attn_inverse).astype(jnp.bfloat16)
    mixed = (attn_hat * up).astype(jnp.bfloat16)
    out_ref[0] = (seq[...].astype(jnp.float32) + dot(mixed, w_out[...])).astype(
        jnp.bfloat16
    )
    dq[...] = jnp.zeros_like(dq)
    dk[...] = jnp.zeros_like(dk)
    dv[...] = jnp.zeros_like(dv)

    gather(dg, ds_, dr, key_back, query_back)

    def d_pre(part, grad):
        halfs = pre[part]
        return (grad * slope_half(halfs, jnp.tanh(halfs))).astype(jnp.bfloat16)

    normalized = jnp.zeros((rows, width), jnp.float32)
    for part, grad in enumerate((dup, dv, dq, dk)):
        piece = d_pre(part, grad[...])
        normalized += dot_nt(piece, w_in[:, part * width : (part + 1) * width])
    xhat, inverse = layer_statistics(seq[...].astype(jnp.float32))
    attn[...] = og_ref[0].astype(jnp.float32) + norm_backward_pass(
        normalized, xhat, inverse
    )

    def back_block(t):
        block = attn[0:BROWS, :]
        for s in range(1, NBLK):
            other = attn[s * BROWS : (s + 1) * BROWS, :]
            block = choose(arrives(s, t), other, block)
        return block.astype(jnp.bfloat16)

    for k in range(tabs):
        t = lax.rem(tab + k, tabs)
        if k == 0:
            back_in[tab] = back_block(t)
        else:
            back_out[t] = back_block(t)
            route_copy(back_out, back_in, bs, br, t).start()
    for k in range(1, tabs):
        route_wait(back_out, back_in, bs, br, lax.rem(tab + k, tabs))
    for p in range(NBLK):
        block = back_in[0]
        for t in range(1, tabs):
            block = choose(dests[0, tab, p] == t, back_in[t], block)
        grads_ref[p * BROWS : (p + 1) * BROWS, :] = block


def body(n, tabs, table, row_ids, dests, slots, lengths, tile_mask, w_in, w_out, og):
    count = row_ids.shape[2]
    width = w_out.shape[0]
    table_rows = table.shape[2]
    cut = 512
    bf16, f32 = jnp.bfloat16, jnp.float32
    vmem = pl.BlockSpec(memory_space=pltpu.VMEM)
    smem = pl.BlockSpec(memory_space=pltpu.SMEM)
    ids_spec = pl.BlockSpec((1, 1, count), lambda i: (0, 0, 0))
    tile_spec = pl.BlockSpec((1, 1, cut, width), lambda i: (0, 0, i, 0))
    rows_spec = pl.BlockSpec((count, width), lambda i: (0, 0))
    looked = pl.pallas_call(
        lookup_kernel,
        out_shape=jax.ShapeDtypeStruct((count, width), bf16),
        grid=(table_rows // cut,),
        in_specs=[ids_spec, tile_spec],
        out_specs=rows_spec,
        scratch_shapes=[pltpu.VMEM((count, width), f32)],
        name="lookup",
    )(row_ids, table)
    dma = pltpu.SemaphoreType.DMA
    layer_out, row_grads = pl.pallas_call(
        functools.partial(layer_kernel, n, tabs),
        out_shape=(
            jax.ShapeDtypeStruct((1, count, width), bf16),
            jax.ShapeDtypeStruct((count, width), bf16),
        ),
        in_specs=[smem] * 4 + [vmem] * 4,
        out_specs=(vmem, vmem),
        scratch_shapes=[
            pltpu.VMEM((n, count, width), bf16),
            pltpu.VMEM((n, count, width), bf16),
            pltpu.VMEM((3, n, count, width), bf16),
            pltpu.VMEM((n, H, count, count), bf16),
            pltpu.VMEM((n, H, count, count), bf16),
            pltpu.VMEM((n, H, count, count), bf16),
            pltpu.VMEM((4, count, width), f32),
            pltpu.VMEM((count, width), f32),
            pltpu.VMEM((count, width), bf16),
            pltpu.VMEM((count, width), f32),
            pltpu.VMEM((count, width), f32),
            pltpu.VMEM((count, width), f32),
            pltpu.VMEM((count, width), f32),
            pltpu.VMEM((count, 128), jnp.int32),
            pltpu.VMEM((tabs, BROWS, width), bf16),
            pltpu.VMEM((tabs, BROWS, width), bf16),
            pltpu.VMEM((tabs, BROWS, width), bf16),
            pltpu.VMEM((tabs, BROWS, width), bf16),
            dma((3, n)),
            dma((n,)),
            dma((3, n)),
            dma((n,)),
            dma((tabs,)),
            dma((tabs,)),
            dma((tabs,)),
            dma((tabs,)),
        ],
        compiler_params=pltpu.CompilerParams(
            collective_id=0, has_side_effects=True, vmem_limit_bytes=60 * 1024 * 1024
        ),
        name="layer",
    )(dests, slots, lengths, tile_mask, looked, w_in, w_out, og)
    table_grad = pl.pallas_call(
        scatter_kernel,
        out_shape=jax.ShapeDtypeStruct((1, 1, table_rows, width), bf16),
        grid=(table_rows // cut,),
        in_specs=[ids_spec, rows_spec],
        out_specs=tile_spec,
        name="table_grad",
    )(row_ids, row_grads)
    return layer_out, table_grad


def solution(mesh):
    in_specs = (
        P("ctx", "tab", None, None),
        P("ctx", "tab", None),
        P("ctx", None, None),
        P("ctx", None, None),
        P("tab", None),
        P("tab", None, None),
        P(),
        P(),
        P("tab", "ctx", None),
    )
    out_specs = (P("tab", "ctx", None), P("ctx", "tab", None, None))
    return jax.shard_map(
        functools.partial(body, mesh.shape["ctx"], mesh.shape["tab"]),
        mesh=mesh,
        in_specs=in_specs,
        out_specs=out_specs,
        check_vma=False,
    )
```

time: 303 us -> 101 us (0.33)
  waiting for transfers between devices: 156 us -> 0 us
  Pallas kernels: 0 us -> 99 us
  matrix products: 68.8 us -> 0 us
  local copies, waits for them, and re-layouts: 33.7 us -> 0.71 us
  other arithmetic: 17.4 us -> 0 us
  between operations: 15.3 us -> 0.65 us
  starting transfers between devices: 9.57 us -> 0 us
    all_gather x4 -> x0, waiting for transfers between devices: 147 us -> none  [the longest x1 50.5 us: body(): value_in = lax.all_gather(value_part, 'ctx', axis=0, tiled=True)]
    pallas_call x0 -> x3, Pallas kernels: none -> 99 us  [the longest x1 86.5 us: body(): pl.pallas_call(functools.partial(layer_kernel, n, tabs), out_shape=(jax.S...]
    dot_general x18 -> x0, matrix products: 68.8 us -> none  [the longest x1 11 us: query_compute(): jnp.einsum('hqk,khd->qhd', d_scores, key_heads, preferred_element_type=jn...]
    another operation x5 -> x0, local copies, waits for them, and re-layouts: 16.1 us -> none
    all_to_all x2 -> x0, starting transfers between devices: 9.45 us -> none  [the longest x1 5.16 us: body(): lax.all_to_all(returning, 'tab', split_axis=0, concat_axis=0, tiled=True)]
    all_to_all x2 -> x0, waiting for transfers between devices: 7.88 us -> none  [the longest x1 4.89 us: body(): lax.all_to_all(outgoing, 'tab', split_axis=0, concat_axis=0, tiled=True)]
    cond x8 -> x0, local copies, waits for them, and re-layouts: 7.37 us -> none  [the longest x2 4.09 us: body(): lax.cond(jnp.any(key_allowed > 0.5), key_compute, lambda totals: totals,...]
    reshape x1 -> x0, other arithmetic: 5.93 us -> none  [body(): table_grad.reshape(1, 1, table.shape[2], model_width)]
  transfers between devices with their start and end apart: 6 -> 0, of which waited for: 6 -> 0; matrix products, arithmetic and copies ran while one was open for 17% -> 0% of each run, Pallas kernels for 0% -> 0%
where the time goes in v1:
time: 101 us; the launch traced here: 100 us
  Pallas kernels  99 us (98%)
    pallas_call x1, Pallas kernels, body(): pl.pallas_call(functools.partial(layer_kernel, n, tabs), out_shape=(jax.S...  86.5 us
    pallas_call x1, Pallas kernels, body(): pl.pallas_call(lookup_kernel, out_shape=jax.ShapeDtypeStruct((count, widt...  6.76 us
    pallas_call x1, Pallas kernels, body(): pl.pallas_call(scatter_kernel, out_shape=jax.ShapeDtypeStruct((1, 1, tabl...  5.72 us

profile of v1, /device:TPU:1, one launch (start us, length us, event | category | flops | bytes accessed | tf_op | source)
XLA Modules:
  0.0 100.3 jit_solution(10944239689996436466)
XLA Ops:
  0.6 6.8 %lookup.1.rows_ref = bf16[256,512]{1,0:T(8,128)(2,1)} custom-call(s32[1,1,256]{2,1,0:T(1,128)} %ids_ref.3, bf16[1,1,4096,512]{3,2,1,0:T(8,128)(2,1)} %table_ref.1), custom_call_target="tpu_custom_call" | custom-call | tf_op jit(solution)/shard_map/lookup/pallas_call | solution.py:428
  7.4 86.5 %layer.1 = (bf16[1,256,512]{2,1,0:T(8,128)(2,1)}, bf16[256,512]{1,0:T(8,128)(2,1)}) custom-call(s32[1,4,4]{2,1,0:T(4,128)} %dests.1, s32[1,4,4]{2,1,0:T(4,128)} %slots.1, s32[1,16]{1,0:T(1,128)} %lengths.1, s32[1,32,32]{2,1,0:T(8,128)} %tiles.1, bf16[256,512]{1,0:T(8,128)(2,1)} %lookup.1.rows_ref, bf16[512,2048]{1,0:T(8,128)(2,1)} %w_in.1, ...), custom_call_target="tpu_custom_call" | custom-call | tf_op jit(solution)/shard_map/layer/pallas_call | solution.py:438
  93.9 0.0 copy-start
  93.9 5.7 %table_grad.1 = bf16[1,1,4096,512]{3,2,1,0:T(8,128)(2,1)} custom-call(s32[1,1,256]{2,1,0:T(1,128)} %ids_ref.3, bf16[256,512]{1,0:T(8,128)(2,1)} %get-tuple-element.5.grads_ref), custom_call_target="tpu_custom_call" | custom-call | tf_op jit(solution)/shard_map/table_grad/pallas_call | solution.py:479
  99.6 0.0 copy-done
  99.6 0.7 copy.12
Async XLA Ops:
  93.9 5.7 %copy-start = (bf16[1,256,512]{2,1,0:T(8,128)(2,1)S(1)}, bf16[1,256,512]{2,1,0:T(8,128)(2,1)}, u32[]{:S(2)}) copy-start(bf16[1,256,512]{2,1,0:T(8,128)(2,1)} %get-tuple-element.8) | copy-start | bytes 786436

commit v2 on v1

--- a/solution.py
+++ b/solution.py
@@ -47,7 +47,7 @@
     return (0.5 + 0.5 * tanh) * (1.0 + half * (1.0 - tanh))
 
 
-def lookup_kernel(ids_ref, table_ref, out_ref, acc):
+def lookup_kernel(ids_ref, table_ref, out_ref, acc, column):
     step = pl.program_id(0)
     rows = table_ref.shape[2]
     count = ids_ref.shape[2]
@@ -55,13 +55,15 @@
     @pl.when(step == 0)
     def _():
         acc[...] = jnp.zeros_like(acc)
-
-    base = step * rows
-    row = lax.broadcasted_iota(jnp.int32, (rows, count), 0) + base
-    pick = jnp.where(row == ids_ref[0], 1.0, 0.0).astype(jnp.bfloat16)
-    acc[...] += lax.dot_general(
-        pick, table_ref[0, 0], TN, preferred_element_type=jnp.float32
-    )
+        line = jnp.broadcast_to(ids_ref[0].astype(jnp.float32), (128, count))
+        column[...] = line.T.astype(jnp.int32)
+
+    lane = lax.broadcasted_iota(jnp.int32, (count, 128), 1) + step * rows
+    picks = [
+        jnp.where(column[...] == lane + k * 128, 1.0, 0.0).astype(jnp.bfloat16)
+        for k in range(rows // 128)
+    ]
+    acc[...] += dot(jnp.concatenate(picks, axis=1), table_ref[0, 0])
 
     @pl.when(step == pl.num_programs(0) - 1)
     def _():
@@ -102,6 +104,10 @@
     dk,
     dv,
     dup,
+    dm,
+    up,
+    xhat,
+    xinv,
     startq,
     route_out,
     route_in,
@@ -188,6 +194,8 @@
     for k in range(1, tabs):
         route_copy(route_out, route_in, rs, rr, lax.rem(tab + k, tabs)).start()
 
+    dm[...] = dot_nt(og_ref[0], w_out[...])
+
     def starts_of(pos):
         end = jnp.int32(0)
         start = jnp.zeros_like(pos)
@@ -196,46 +204,47 @@
             start = jnp.where(pos >= end, end, start)
         return start
 
-    def positions(s, shape, dim):
-        local = lax.broadcasted_iota(jnp.int32, shape, dim)
-        return local + jnp.where(local < half, s * half, (2 * n - 1 - s) * half - half)
-
-    startq[...] = starts_of(positions(me, (rows, 128), 0))
+    def base_of(s, side):
+        return (2 * n - 1 - s) * half if side else s * half
+
+    for side in range(2):
+        local = lax.broadcasted_iota(jnp.int32, (half, 128), 0)
+        startq[side * half : (side + 1) * half, :] = starts_of(local + base_of(me, side))
     attn[...] = jnp.zeros_like(attn)
 
-    def tile_id(s, a):
-        if a < per_half:
-            return s * per_half + a
-        return (2 * n - 1 - s) * per_half + a - per_half
-
-    count = 2 * per_half
-
     def tile_rows(pick):
-        block = lax.broadcasted_iota(jnp.int32, (BROWS, rows), 1) // BROWS
+        block = lax.broadcasted_iota(jnp.int32, (BROWS, half), 1) // BROWS
         stripes = []
-        for a in range(count):
-            line = jnp.zeros((BROWS, rows), jnp.int32)
-            for b in range(count):
+        for a in range(per_half):
+            line = jnp.full((BROWS, half), pick(a, 0))
+            for b in range(1, per_half):
                 line = jnp.where(block == b, pick(a, b), line)
             stripes.append(line)
         return jnp.concatenate(stripes, axis=0) > 0
 
-    def query_mask(s):
-        own = positions(me, (rows, rows), 0)
-        other = positions(s, (rows, rows), 1)
-        first = jnp.broadcast_to(startq[:, 0:1], (rows, rows))
-        on = tile_rows(lambda a, b: tiles[0, tile_id(me, a), tile_id(s, b)])
+    def query_mask(s, mine, theirs):
+        at, to = base_of(me, mine), base_of(s, theirs)
+        own = lax.broadcasted_iota(jnp.int32, (half, half), 0) + at
+        other = lax.broadcasted_iota(jnp.int32, (half, half), 1) + to
+        first = startq[mine * half : (mine + 1) * half, :]
+        at, to = at // BROWS, to // BROWS
+        on = tile_rows(lambda a, b: tiles[0, at + a, to + b])
         return jnp.where((other <= own) & (other >= first) & on, 1.0, 0.0)
 
-    def key_mask(s):
-        own = positions(me, (rows, rows), 0)
-        other = positions(s, (rows, rows), 1)
-        first = starts_of(positions(s, (1, rows), 1))
-        on = tile_rows(lambda a, b: tiles[0, tile_id(s, b), tile_id(me, a)])
+    def key_mask(s, mine, theirs):
+        at, to = base_of(me, mine), base_of(s, theirs)
+        own = lax.broadcasted_iota(jnp.int32, (half, half), 0) + at
+        other = lax.broadcasted_iota(jnp.int32, (half, half), 1) + to
+        first = starts_of(lax.broadcasted_iota(jnp.int32, (1, half), 1) + to)
+        at, to = at // BROWS, to // BROWS
+        on = tile_rows(lambda a, b: tiles[0, to + b, at + a])
         return jnp.where((own <= other) & (own >= first) & on, 1.0, 0.0)
 
-    def take(buf, part, s, h):
-        return buf[part, s, :, h * hd : (h + 1) * hd]
+    def side_rows(side):
+        return slice(side * half, (side + 1) * half)
+
+    def take(part, s, side, h):
+        return vqk[part, s, side_rows(side), h * hd : (h + 1) * hd]
 
     def project(s):
         block = xg[s]
@@ -244,38 +253,62 @@
             value = dot(block, w_in[:, lo : lo + width])
             vqk[part, s] = silu_half(0.5 * value).astype(jnp.bfloat16)
 
+    def quads(s):
+        return (
+            (s <= me, 0, 0, 1, 1),
+            (s >= n - 1 - me, 1, 0, 0, 1),
+            (s >= me, 1, 1, 0, 0),
+        )
+
     def forward(s):
         project(s)
-        mask = query_mask(s)
-        for h in range(H):
-            cut = slice(h * hd, (h + 1) * hd)
-            halfs = dot_nt(take(vqk, 1, me, h), take(vqk, 2, s, h)) * (0.5 * scale)
-            tanh = jnp.tanh(halfs)
-            probs = (halfs * (1.0 + tanh) * mask).astype(jnp.bfloat16)
-            gq[s, h] = (slope_half(halfs, tanh) * (mask * scale)).astype(jnp.bfloat16)
-            attn[:, cut] += dot(probs, take(vqk, 0, s, h))
-        mask = key_mask(s)
-        for h in range(H):
-            halfs = dot_nt(take(vqk, 2, me, h), take(vqk, 1, s, h)) * (0.5 * scale)
-            tanh = jnp.tanh(halfs)
-            pk[s, h] = (halfs * (1.0 + tanh) * mask).astype(jnp.bfloat16)
-            gk[s, h] = (slope_half(halfs, tanh) * (mask * scale)).astype(jnp.bfloat16)
+        for i, (when, qm, kt, km, qt) in enumerate(quads(s)):
+
+            @pl.when(when)
+            def _(i=i, qm=qm, kt=kt, km=km, qt=qt):
+                mask = query_mask(s, qm, kt)
+                scaled = mask * scale
+                mask_k = key_mask(s, km, qt)
+                scaled_k = mask_k * scale
+                for h in range(H):
+                    cut = slice(h * hd, (h + 1) * hd)
+                    halfs = dot_nt(take(1, me, qm, h), take(2, s, kt, h)) * (0.5 * scale)
+                    tanh = jnp.tanh(halfs)
+                    probs = (halfs * (1.0 + tanh) * mask).astype(jnp.bfloat16)
+                    gq[i, s, h] = (slope_half(halfs, tanh) * scaled).astype(jnp.bfloat16)
+                    attn[side_rows(qm), cut] += dot(probs, take(0, s, kt, h))
+                    halfs = dot_nt(take(2, me, km, h), take(1, s, qt, h)) * (0.5 * scale)
+                    tanh = jnp.tanh(halfs)
+                    pk[i, s, h] = (halfs * (1.0 + tanh) * mask_k).astype(jnp.bfloat16)
+                    gk[i, s, h] = (slope_half(halfs, tanh) * scaled_k).astype(jnp.bfloat16)
 
     def query_back(s):
-        for h in range(H):
-            cut = slice(h * hd, (h + 1) * hd)
-            slope = gq[s, h].astype(jnp.float32)
-            dsc = dot_nt(dg[me, :, cut], take(vqk, 0, s, h)) * slope
-            dq[:, cut] += dot(dsc.astype(jnp.bfloat16), take(vqk, 2, s, h))
+        for i, (when, qm, kt, _, _) in enumerate(quads(s)):
+
+            @pl.when(when)
+            def _(i=i, qm=qm, kt=kt):
+                for h in range(H):
+                    cut = slice(h * hd, (h + 1) * hd)
+                    slope = gq[i, s, h].astype(jnp.float32)
+                    dsc = dot_nt(dg[me, side_rows(qm), cut], take(0, s, kt, h)) * slope
+                    dq[side_rows(qm), cut] += dot(
+                        dsc.astype(jnp.bfloat16), take(2, s, kt, h)
+                    )
 
     def key_back(s):
-        for h in range(H):
-            cut = slice(h * hd, (h + 1) * hd)
-            grad = dg[s, :, cut]
-            slope = gk[s, h].astype(jnp.float32)
-            dsc = dot_nt(take(vqk, 0, me, h), grad) * slope
-            dk[:, cut] += dot(dsc.astype(jnp.bfloat16), take(vqk, 1, s, h))
-            dv[:, cut] += dot(pk[s, h], grad)
+        for i, (when, _, _, km, qt) in enumerate(quads(s)):
+
+            @pl.when(when)
+            def _(i=i, km=km, qt=qt):
+                for h in range(H):
+                    cut = slice(h * hd, (h + 1) * hd)
+                    grad = dg[s, side_rows(qt), cut]
+                    slope = gk[i, s, h].astype(jnp.float32)
+                    dsc = dot_nt(take(0, me, km, h), grad) * slope
+                    dk[side_rows(km), cut] += dot(
+                        dsc.astype(jnp.bfloat16), take(1, s, qt, h)
+                    )
+                    dv[side_rows(km), cut] += dot(pk[i, s, h], grad)
 
     def gather(buf, send, recv, compute, filler):
         def copy(s, way):
@@ -320,8 +353,7 @@
                 ways(zz, lambda c: c.start())
                 compute(s)
 
-            if filler is not None:
-                filler(j)
+            filler(j)
             before = level(j - 1)
 
             @pl.when((j > 0) & (before >= 0) & (before < levels))
@@ -356,39 +388,61 @@
             block = choose(arrives(s, t), route_in[t], block)
         seq[s * BROWS : (s + 1) * BROWS, :] = block
 
-    xhat, inverse = layer_statistics(seq[...].astype(jnp.float32))
-    xg[me] = xhat.astype(jnp.bfloat16)
-
-    gather(xg, xs, xr, forward, None)
-
-    for part in range(4):
-        pre[part] = 0.5 * dot(xg[me], w_in[:, part * width : (part + 1) * width])
-    up = silu_half(pre[0]).astype(jnp.bfloat16).astype(jnp.float32)
+    normal, inverse = layer_statistics(seq[...].astype(jnp.float32))
+    xg[me] = normal.astype(jnp.bfloat16)
+    xhat[...] = normal
+    xinv[...] = jnp.broadcast_to(inverse, xinv.shape)
+
+    def part_of(part):
+        return w_in[:, part * width : (part + 1) * width]
+
+    def own_rows(j):
+        @pl.when(j == 0)
+        def _():
+            for part in range(4):
+                halfs = 0.5 * dot(xg[me], part_of(part))
+                tanh = jnp.tanh(halfs)
+                pre[part] = slope_half(halfs, tanh)
+                if part == 0:
+                    act = (halfs * (1.0 + tanh)).astype(jnp.bfloat16)
+                    up[...] = act.astype(jnp.float32)
+
+    gather(xg, xs, xr, forward, own_rows)
+
     attn_hat, attn_inverse = layer_statistics(attn[...])
-    dmixed = dot_nt(og_ref[0], w_out[...])
-    dup[...] = dmixed * attn_hat
-    dg[me] = norm_backward_pass(dmixed * up, attn_hat, attn_inverse).astype(jnp.bfloat16)
-    mixed = (attn_hat * up).astype(jnp.bfloat16)
-    out_ref[0] = (seq[...].astype(jnp.float32) + dot(mixed, w_out[...])).astype(
+    dg[me] = norm_backward_pass(dm[...] * up[...], attn_hat, attn_inverse).astype(
         jnp.bfloat16
     )
+    attn[...] = attn_hat
     dq[...] = jnp.zeros_like(dq)
     dk[...] = jnp.zeros_like(dk)
     dv[...] = jnp.zeros_like(dv)
 
-    gather(dg, ds_, dr, key_back, query_back)
-
     def d_pre(part, grad):
-        halfs = pre[part]
-        return (grad * slope_half(halfs, jnp.tanh(halfs))).astype(jnp.bfloat16)
-
-    normalized = jnp.zeros((rows, width), jnp.float32)
-    for part, grad in enumerate((dup, dv, dq, dk)):
-        piece = d_pre(part, grad[...])
-        normalized += dot_nt(piece, w_in[:, part * width : (part + 1) * width])
-    xhat, inverse = layer_statistics(seq[...].astype(jnp.float32))
+        return dot_nt((grad * pre[part]).astype(jnp.bfloat16), part_of(part))
+
+    def own_back(j):
+        @pl.when(j == 0)
+        def _():
+            attn_hat = attn[...]
+            mixed = (attn_hat * up[...]).astype(jnp.bfloat16)
+            out_ref[0] = (seq[...].astype(jnp.float32) + dot(mixed, w_out[...])).astype(
+                jnp.bfloat16
+            )
+            dup[...] = d_pre(0, dm[...] * attn_hat)
+
+        for k in range(n // (2 * levels)):
+            query_back(j * (n // (2 * levels)) + k)
+
+        @pl.when(j == 2 * levels - 1)
+        def _():
+            dup[...] += d_pre(2, dq[...])
+
+    gather(dg, ds_, dr, key_back, own_back)
+
+    normalized = dup[...] + d_pre(1, dv[...]) + d_pre(3, dk[...])
     attn[...] = og_ref[0].astype(jnp.float32) + norm_backward_pass(
-        normalized, xhat, inverse
+        normalized, xhat[...], xinv[:, 0:1]
     )
 
     def back_block(t):
@@ -418,7 +472,7 @@
     count = row_ids.shape[2]
     width = w_out.shape[0]
     table_rows = table.shape[2]
-    cut = 512
+    cut = 1024
     bf16, f32 = jnp.bfloat16, jnp.float32
     vmem = pl.BlockSpec(memory_space=pltpu.VMEM)
     smem = pl.BlockSpec(memory_space=pltpu.SMEM)
@@ -431,7 +485,10 @@
         grid=(table_rows // cut,),
         in_specs=[ids_spec, tile_spec],
         out_specs=rows_spec,
-        scratch_shapes=[pltpu.VMEM((count, width), f32)],
+        scratch_shapes=[
+            pltpu.VMEM((count, width), f32),
+            pltpu.VMEM((count, 128), jnp.int32),
+        ],
         name="lookup",
     )(row_ids, table)
     dma = pltpu.SemaphoreType.DMA
@@ -447,9 +504,9 @@
             pltpu.VMEM((n, count, width), bf16),
             pltpu.VMEM((n, count, width), bf16),
             pltpu.VMEM((3, n, count, width), bf16),
-            pltpu.VMEM((n, H, count, count), bf16),
-            pltpu.VMEM((n, H, count, count), bf16),
-            pltpu.VMEM((n, H, count, count), bf16),
+            pltpu.VMEM((3, n, H, count // 2, count // 2), bf16),
+            pltpu.VMEM((3, n, H, count // 2, count // 2), bf16),
+            pltpu.VMEM((3, n, H, count // 2, count // 2), bf16),
             pltpu.VMEM((4, count, width), f32),
             pltpu.VMEM((count, width), f32),
             pltpu.VMEM((count, width), bf16),
@@ -457,6 +514,10 @@
             pltpu.VMEM((count, width), f32),
             pltpu.VMEM((count, width), f32),
             pltpu.VMEM((count, width), f32),
+            pltpu.VMEM((count, width), f32),
+            pltpu.VMEM((count, width), f32),
+            pltpu.VMEM((count, width), f32),
+            pltpu.VMEM((count, 128), f32),
             pltpu.VMEM((count, 128), jnp.int32),
             pltpu.VMEM((tabs, BROWS, width), bf16),
             pltpu.VMEM((tabs, BROWS, width), bf16),

time: 101 us -> 95.5 us (0.946)
  Pallas kernels: 99 us -> 93.9 us
    pallas_call x1, Pallas kernels: 6.76 us -> 4.71 us  [body(): pl.pallas_call(lookup_kernel, out_shape=jax.ShapeDtypeStruct((count, widt...]
    pallas_call x1, Pallas kernels: 86.5 us -> 85 us  [body(): pl.pallas_call(functools.partial(layer_kernel, n, tabs), out_shape=(jax.S...]
    pallas_call x1, Pallas kernels: 5.72 us -> 4.28 us  [body(): pl.pallas_call(scatter_kernel, out_shape=jax.ShapeDtypeStruct((1, 1, tabl...]
where the time goes in v2:
time: 95.5 us; the launch traced here: 95.3 us
  Pallas kernels  93.9 us (98%)
    pallas_call x1, Pallas kernels, body(): pl.pallas_call(functools.partial(layer_kernel, n, tabs), out_shape=(jax.S...  85 us
    pallas_call x1, Pallas kernels, body(): pl.pallas_call(lookup_kernel, out_shape=jax.ShapeDtypeStruct((count, widt...  4.71 us
    pallas_call x1, Pallas kernels, body(): pl.pallas_call(scatter_kernel, out_shape=jax.ShapeDtypeStruct((1, 1, tabl...  4.28 us

profile of v2, /device:TPU:1, one launch (start us, length us, event | category | flops | bytes accessed | tf_op | source)
XLA Modules:
  0.0 95.3 jit_solution(5178474987964590536)
XLA Ops:
  0.6 4.7 %lookup.1.rows_ref = bf16[256,512]{1,0:T(8,128)(2,1)} custom-call(s32[1,1,256]{2,1,0:T(1,128)} %ids_ref.3, bf16[1,1,4096,512]{3,2,1,0:T(8,128)(2,1)} %table_ref.1), custom_call_target="tpu_custom_call" | custom-call | tf_op jit(solution)/shard_map/lookup/pallas_call | solution.py:482
  5.3 85.0 %layer.1 = (bf16[1,256,512]{2,1,0:T(8,128)(2,1)}, bf16[256,512]{1,0:T(8,128)(2,1)}) custom-call(s32[1,4,4]{2,1,0:T(4,128)} %dests.1, s32[1,4,4]{2,1,0:T(4,128)} %slots.1, s32[1,16]{1,0:T(1,128)} %lengths.1, s32[1,32,32]{2,1,0:T(8,128)} %tiles.1, bf16[256,512]{1,0:T(8,128)(2,1)} %lookup.1.rows_ref, bf16[512,2048]{1,0:T(8,128)(2,1)} %w_in.1, ...), custom_call_target="tpu_custom_call" | custom-call | tf_op jit(solution)/shard_map/layer/pallas_call | solution.py:495
  90.3 0.0 copy-start
  90.3 4.3 %table_grad.1 = bf16[1,1,4096,512]{3,2,1,0:T(8,128)(2,1)} custom-call(s32[1,1,256]{2,1,0:T(1,128)} %ids_ref.3, bf16[256,512]{1,0:T(8,128)(2,1)} %get-tuple-element.5.grads_ref), custom_call_target="tpu_custom_call" | custom-call | tf_op jit(solution)/shard_map/table_grad/pallas_call | solution.py:540
  94.6 0.0 copy-done
  94.6 0.7 copy.12
Async XLA Ops:
  90.3 4.3 %copy-start = (bf16[1,256,512]{2,1,0:T(8,128)(2,1)S(1)}, bf16[1,256,512]{2,1,0:T(8,128)(2,1)}, u32[]{:S(2)}) copy-start(bf16[1,256,512]{2,1,0:T(8,128)(2,1)} %get-tuple-element.8) | copy-start | bytes 786436

commit v3 on v2

--- a/solution.py
+++ b/solution.py
@@ -47,35 +47,21 @@
     return (0.5 + 0.5 * tanh) * (1.0 + half * (1.0 - tanh))
 
 
-def lookup_kernel(ids_ref, table_ref, out_ref, acc, column):
-    step = pl.program_id(0)
-    rows = table_ref.shape[2]
+def scatter_kernel(ids_ref, grads_ref, out_ref, held, sems):
     count = ids_ref.shape[2]
-
-    @pl.when(step == 0)
-    def _():
-        acc[...] = jnp.zeros_like(acc)
-        line = jnp.broadcast_to(ids_ref[0].astype(jnp.float32), (128, count))
-        column[...] = line.T.astype(jnp.int32)
-
-    lane = lax.broadcasted_iota(jnp.int32, (count, 128), 1) + step * rows
-    picks = [
-        jnp.where(column[...] == lane + k * 128, 1.0, 0.0).astype(jnp.bfloat16)
-        for k in range(rows // 128)
-    ]
-    acc[...] += dot(jnp.concatenate(picks, axis=1), table_ref[0, 0])
-
-    @pl.when(step == pl.num_programs(0) - 1)
-    def _():
-        out_ref[...] = acc[...].astype(out_ref.dtype)
-
-
-def scatter_kernel(ids_ref, grads_ref, out_ref):
-    rows = out_ref.shape[2]
-    count = ids_ref.shape[2]
-    row = lax.broadcasted_iota(jnp.int32, (rows, count), 0) + pl.program_id(0) * rows
-    pick = jnp.where(row == ids_ref[0], 1.0, 0.0).astype(jnp.bfloat16)
-    out_ref[0, 0] = dot(pick, grads_ref[...]).astype(out_ref.dtype)
+    pieces = sems.shape[0]
+    rows = held.shape[0] // pieces
+    copies = []
+    for i in range(pieces):
+        row = lax.broadcasted_iota(jnp.int32, (rows, count), 0) + i * rows
+        pick = jnp.where(row == ids_ref[0], 1.0, 0.0).astype(jnp.bfloat16)
+        at = pl.ds(i * rows, rows)
+        held[at, :] = dot(pick, grads_ref[...]).astype(held.dtype)
+        copy = pltpu.make_async_copy(held.at[at], out_ref.at[0, 0, at], sems.at[i])
+        copy.start()
+        copies.append(copy)
+    for copy in copies:
+        copy.wait()
 
 
 def layer_kernel(
@@ -85,9 +71,10 @@
     slots,
     lengths,
     tiles,
-    rows_ref,
-    w_in,
-    w_out,
+    ids_ref,
+    table_ref,
+    w_in_ref,
+    w_out_ref,
     og_ref,
     out_ref,
     grads_ref,
@@ -121,18 +108,39 @@
     rr,
     bs,
     br,
+    held,
+    w_in,
+    w_out,
+    looked,
+    local_sems,
 ):
     me = lax.axis_index("ctx")
     tab = lax.axis_index("tab")
     levels = n // FAST
     z = me // FAST
     x = me % FAST
-    rows = rows_ref.shape[0]
-    width = rows_ref.shape[1]
+    rows, width = looked.shape
     half = rows // 2
     per_half = half // BROWS
     hd = width // H
     scale = hd ** (-0.5)
+
+    pieces = local_sems.shape[0] - 2
+    piece = held.shape[0] // pieces
+    loads = [
+        pltpu.make_async_copy(
+            table_ref.at[0, 0, pl.ds(i * piece, piece)],
+            held.at[pl.ds(i * piece, piece)],
+            local_sems.at[i],
+        )
+        for i in range(pieces)
+    ]
+    load_out = pltpu.make_async_copy(w_out_ref, w_out, local_sems.at[pieces])
+    load_in = pltpu.make_async_copy(w_in_ref, w_in, local_sems.at[pieces + 1])
+    for load in loads:
+        load.start()
+    load_out.start()
+    load_in.start()
 
     barrier = pltpu.get_barrier_semaphore()
 
@@ -151,14 +159,32 @@
     lax.fori_loop(1, n, greet_ctx, 0)
     lax.fori_loop(1, tabs, greet_tab, 0)
 
+    line = jnp.broadcast_to(ids_ref[0], (rows, rows))
+    at_row = lax.broadcasted_iota(jnp.int32, (rows, rows), 0)
+    at_lane = lax.broadcasted_iota(jnp.int32, (rows, rows), 1)
+    column = jnp.where(at_row == at_lane, line, 0).astype(jnp.float32)
+    column = jnp.sum(column, axis=1, keepdims=True)
+    column = jnp.broadcast_to(column, (rows, 128)).astype(jnp.int32)
+    lane = lax.broadcasted_iota(jnp.int32, (rows, 128), 1)
+    found = jnp.zeros((rows, width), jnp.float32)
+    for i, load in enumerate(loads):
+        load.wait()
+        picks = [
+            jnp.where(column == lane + (i * piece + k * 128), 1.0, 0.0)
+            for k in range(piece // 128)
+        ]
+        pick = jnp.concatenate(picks, axis=1).astype(jnp.bfloat16)
+        found += dot(pick, held[pl.ds(i * piece, piece), :])
+    looked[...] = found.astype(jnp.bfloat16)
+
     def choose(hit, block, other):
         on = jnp.full(block.shape, hit.astype(jnp.int32)) > 0
         return jnp.where(on, block, other)
 
     def block_for(t):
-        block = rows_ref[0:BROWS, :]
+        block = looked[0:BROWS, :]
         for p in range(1, NBLK):
-            other = rows_ref[p * BROWS : (p + 1) * BROWS, :]
+            other = looked[p * BROWS : (p + 1) * BROWS, :]
             block = choose(dests[0, tab, p] == t, other, block)
         return block
 
@@ -194,6 +220,7 @@
     for k in range(1, tabs):
         route_copy(route_out, route_in, rs, rr, lax.rem(tab + k, tabs)).start()
 
+    load_out.wait()
     dm[...] = dot_nt(og_ref[0], w_out[...])
 
     def starts_of(pos):
@@ -310,68 +337,98 @@
                     )
                     dv[side_rows(km), cut] += dot(pk[i, s, h], grad)
 
-    def gather(buf, send, recv, compute, filler):
-        def copy(s, way):
-            to = (me - FAST, me + FAST, z * FAST + (FAST - 1 - x))[way]
+    def gather(buf, send, recv, wanted, needed, compute, filler):
+        partner = z * FAST + (FAST - 1 - x)
+
+        def copy(s, side, way):
+            to = (me - FAST, me + FAST, partner)[way]
+            at = pl.ds(side * half, half)
             return pltpu.make_async_remote_copy(
-                src_ref=buf.at[s],
-                dst_ref=buf.at[s],
-                send_sem=send.at[way, s],
-                recv_sem=recv.at[s],
+                src_ref=buf.at[s, at],
+                dst_ref=buf.at[s, at],
+                send_sem=send.at[way, side, s],
+                recv_sem=recv.at[side, s],
                 device_id=(to, tab),
                 device_id_type=MESH,
             )
 
-        def ways(zz, action):
+        def ways(zz, side, action):
             s = zz * FAST + x
 
-            @pl.when((zz >= z) & (z > 0))
+            @pl.when((zz >= z) & (z > 0) & wanted(0, s, side, z))
             def _():
-                action(copy(s, 0))
-
-            @pl.when((zz <= z) & (z < levels - 1))
+                action(copy(s, side, 0))
+
+            @pl.when((zz <= z) & (z < levels - 1) & wanted(1, s, side, z))
             def _():
-                action(copy(s, 1))
-
-            action(copy(s, 2))
-
-        def level(j):
-            far = (j + 1) // 2
-            return z + jnp.where(j % 2 == 1, -far, far)
-
-        def step(j, carry):
-            zz = level(j)
-
-            @pl.when((j < 2 * levels - 1) & (zz >= 0) & (zz < levels))
+                action(copy(s, side, 1))
+
+            @pl.when(needed(partner, s, side))
             def _():
-                s = zz * FAST + x
-
-                @pl.when(j > 0)
+                action(copy(s, side, 2))
+
+        def level(k, i):
+            zz = z + jnp.where(i == 0, -k, k)
+            there = (k >= 0) & (k < levels) & (zz >= 0) & (zz < levels)
+            return zz, there & ((k > 0) | (i == 0))
+
+        def step(k, carry):
+            for i in range(2):
+                zz, there = level(k, i)
+
+                @pl.when(there)
+                def _(i=i, zz=zz):
+                    s = zz * FAST + x
+                    for side in range(2):
+                        got = wanted(1, s, side, z - 1) if i == 0 else wanted(0, s, side, z + 1)
+
+                        @pl.when((k > 0) & got)
+                        def _(side=side):
+                            copy(s, side, 2).wait_recv()
+
+                        ways(zz, side, lambda c: c.start())
+
+            filler(k)
+
+            def own_column(i, carry):
+                zz, there = level(k, i)
+
+                @pl.when(there)
                 def _():
-                    copy(s, 2).wait_recv()
-
-                ways(zz, lambda c: c.start())
-                compute(s)
-
-            filler(j)
-            before = level(j - 1)
-
-            @pl.when((j > 0) & (before >= 0) & (before < levels))
-            def _():
-                s = before * FAST + (FAST - 1 - x)
-                copy(s, 2).wait_recv()
-                compute(s)
-
+                    compute(zz * FAST + x)
+
+                return carry
+
+            def other_column(i, carry):
+                zz, there = level(k - 1, i)
+
+                @pl.when(there)
+                def _():
+                    s = zz * FAST + (FAST - 1 - x)
+                    for side in range(2):
+
+                        @pl.when(needed(me, s, side))
+                        def _(side=side):
+                            copy(s, side, 2).wait_recv()
+
+                    compute(s)
+
+                return carry
+
+            lax.fori_loop(0, 2, own_column, 0)
+            lax.fori_loop(0, 2, other_column, 0)
             return carry
 
-        lax.fori_loop(0, 2 * levels, step, 0)
+        lax.fori_loop(0, levels + 1, step, 0)
 
         def drain(zz, carry):
-            ways(zz, lambda c: c.wait_send())
+            for side in range(2):
+                ways(zz, side, lambda c: c.wait_send())
             return carry
 
         lax.fori_loop(0, levels, drain, 0)
 
+    load_in.wait()
     for k in range(1, tabs):
         route_wait(route_out, route_in, rs, rr, lax.rem(tab + k, tabs))
 
@@ -407,7 +464,10 @@
                     act = (halfs * (1.0 + tanh)).astype(jnp.bfloat16)
                     up[...] = act.astype(jnp.float32)
 
-    gather(xg, xs, xr, forward, own_rows)
+    def always(*_):
+        return me >= 0
+
+    gather(xg, xs, xr, always, always, forward, own_rows)
 
     attn_hat, attn_inverse = layer_statistics(attn[...])
     dg[me] = norm_backward_pass(dm[...] * up[...], attn_hat, attn_inverse).astype(
@@ -431,14 +491,29 @@
             )
             dup[...] = d_pre(0, dm[...] * attn_hat)
 
-        for k in range(n // (2 * levels)):
-            query_back(j * (n // (2 * levels)) + k)
-
-        @pl.when(j == 2 * levels - 1)
+        @pl.when(j < levels)
+        def _():
+            def one(i, carry):
+                query_back(j * FAST + i)
+                return carry
+
+            lax.fori_loop(0, FAST, one, 0)
+
+        @pl.when(j == levels)
         def _():
             dup[...] += d_pre(2, dq[...])
 
-    gather(dg, ds_, dr, key_back, own_back)
+    def needed(d, s, side):
+        if side == 0:
+            return d <= s
+        return (s <= d) | (s >= n - 1 - d)
+
+    def wanted(way, s, side, at):
+        if side == 0:
+            return me >= 0 if way == 0 else me < 0
+        return n - 1 - s <= at * FAST - 1 if way == 0 else me >= 0
+
+    gather(dg, ds_, dr, wanted, needed, key_back, own_back)
 
     normalized = dup[...] + d_pre(1, dv[...]) + d_pre(3, dk[...])
     attn[...] = og_ref[0].astype(jnp.float32) + norm_backward_pass(
@@ -472,25 +547,11 @@
     count = row_ids.shape[2]
     width = w_out.shape[0]
     table_rows = table.shape[2]
-    cut = 1024
+    pieces = 8
     bf16, f32 = jnp.bfloat16, jnp.float32
     vmem = pl.BlockSpec(memory_space=pltpu.VMEM)
     smem = pl.BlockSpec(memory_space=pltpu.SMEM)
-    ids_spec = pl.BlockSpec((1, 1, count), lambda i: (0, 0, 0))
-    tile_spec = pl.BlockSpec((1, 1, cut, width), lambda i: (0, 0, i, 0))
-    rows_spec = pl.BlockSpec((count, width), lambda i: (0, 0))
-    looked = pl.pallas_call(
-        lookup_kernel,
-        out_shape=jax.ShapeDtypeStruct((count, width), bf16),
-        grid=(table_rows // cut,),
-        in_specs=[ids_spec, tile_spec],
-        out_specs=rows_spec,
-        scratch_shapes=[
-            pltpu.VMEM((count, width), f32),
-            pltpu.VMEM((count, 128), jnp.int32),
-        ],
-        name="lookup",
-    )(row_ids, table)
+    hbm = pl.BlockSpec(memory_space=pl.ANY)
     dma = pltpu.SemaphoreType.DMA
     layer_out, row_grads = pl.pallas_call(
         functools.partial(layer_kernel, n, tabs),
@@ -498,7 +559,7 @@
             jax.ShapeDtypeStruct((1, count, width), bf16),
             jax.ShapeDtypeStruct((count, width), bf16),
         ),
-        in_specs=[smem] * 4 + [vmem] * 4,
+        in_specs=[smem] * 4 + [vmem, hbm, hbm, hbm, vmem],
         out_specs=(vmem, vmem),
         scratch_shapes=[
             pltpu.VMEM((n, count, width), bf16),
@@ -523,26 +584,31 @@
             pltpu.VMEM((tabs, BROWS, width), bf16),
             pltpu.VMEM((tabs, BROWS, width), bf16),
             pltpu.VMEM((tabs, BROWS, width), bf16),
-            dma((3, n)),
-            dma((n,)),
-            dma((3, n)),
-            dma((n,)),
+            dma((3, 2, n)),
+            dma((2, n)),
+            dma((3, 2, n)),
+            dma((2, n)),
             dma((tabs,)),
             dma((tabs,)),
             dma((tabs,)),
             dma((tabs,)),
+            pltpu.VMEM((table_rows, width), bf16),
+            pltpu.VMEM(w_in.shape, bf16),
+            pltpu.VMEM(w_out.shape, bf16),
+            pltpu.VMEM((count, width), bf16),
+            dma((pieces + 2,)),
         ],
         compiler_params=pltpu.CompilerParams(
             collective_id=0, has_side_effects=True, vmem_limit_bytes=60 * 1024 * 1024
         ),
         name="layer",
-    )(dests, slots, lengths, tile_mask, looked, w_in, w_out, og)
+    )(dests, slots, lengths, tile_mask, row_ids, table, w_in, w_out, og)
     table_grad = pl.pallas_call(
         scatter_kernel,
         out_shape=jax.ShapeDtypeStruct((1, 1, table_rows, width), bf16),
-        grid=(table_rows // cut,),
-        in_specs=[ids_spec, rows_spec],
-        out_specs=tile_spec,
+        in_specs=[vmem, vmem],
+        out_specs=hbm,
+        scratch_shapes=[pltpu.VMEM((table_rows, width), bf16), dma((pieces,))],
         name="table_grad",
     )(row_ids, row_grads)
     return layer_out, table_grad

time: 95.5 us -> 71.7 us (0.75)
  Pallas kernels: 93.9 us -> 70.2 us
    pallas_call x1, Pallas kernels: 85 us -> 66.8 us  [body(): pl.pallas_call(functools.partial(layer_kernel, n, tabs), out_shape=(jax.S...]
    pallas_call x1 -> x0, Pallas kernels: 4.71 us -> none  [body(): pl.pallas_call(lookup_kernel, out_shape=jax.ShapeDtypeStruct((count, widt...]
where the time goes in v3:
time: 71.7 us; the launch traced here: 71.6 us
  Pallas kernels  70.2 us (98%)
    pallas_call x1, Pallas kernels, body(): pl.pallas_call(functools.partial(layer_kernel, n, tabs), out_shape=(jax.S...  66.8 us
    pallas_call x1, Pallas kernels, body(): pl.pallas_call(scatter_kernel, out_shape=jax.ShapeDtypeStruct((1, 1, tabl...  3.38 us

profile of v3, /device:TPU:1, one launch (start us, length us, event | category | flops | bytes accessed | tf_op | source)
XLA Modules:
  0.0 71.6 jit_solution(15664370740822301418)
XLA Ops:
  0.6 66.8 %layer.1 = (bf16[1,256,512]{2,1,0:T(8,128)(2,1)}, bf16[256,512]{1,0:T(8,128)(2,1)}) custom-call(s32[1,4,4]{2,1,0:T(4,128)} %dests.1, s32[1,4,4]{2,1,0:T(4,128)} %slots.1, s32[1,16]{1,0:T(1,128)} %lengths.1, s32[1,32,32]{2,1,0:T(8,128)} %tiles.1, s32[1,1,256]{2,1,0:T(1,128)} %ids_ref.3, bf16[1,1,4096,512]{3,2,1,0:T(8,128)(2,1)} %table_ref.1, ...), custom_call_target="tpu_custom_call" | custom-call | tf_op jit(solution)/shard_map/layer/pallas_call | solution.py:556
  67.4 0.0 copy-start
  67.4 3.4 %table_grad.1 = bf16[1,1,4096,512]{3,2,1,0:T(8,128)(2,1)} custom-call(s32[1,1,256]{2,1,0:T(1,128)} %ids_ref.3, bf16[256,512]{1,0:T(8,128)(2,1)} %get-tuple-element.5.grads_ref), custom_call_target="tpu_custom_call" | custom-call | tf_op jit(solution)/shard_map/table_grad/pallas_call | solution.py:606
  70.8 0.0 copy-done
  70.8 0.7 copy.12
Async XLA Ops:
  67.4 3.4 %copy-start = (bf16[1,256,512]{2,1,0:T(8,128)(2,1)S(1)}, bf16[1,256,512]{2,1,0:T(8,128)(2,1)}, u32[]{:S(2)}) copy-start(bf16[1,256,512]{2,1,0:T(8,128)(2,1)} %get-tuple-element.8) | copy-start | bytes 786436

commit v4 on v3

--- a/solution.py
+++ b/solution.py
@@ -11,6 +11,7 @@
 BROWS = 64
 NBLK = 4
 FAST = 2
+ALONG = 1
 
 epsilon = 1e-05
 MESH = pl.DeviceIdType.MESH
@@ -47,9 +48,11 @@
     return (0.5 + 0.5 * tanh) * (1.0 + half * (1.0 - tanh))
 
 
-def scatter_kernel(ids_ref, grads_ref, out_ref, held, sems):
+def scatter_kernel(ids_ref, grads_ref, layer_ref, out_ref, layer_out_ref, held, sems):
     count = ids_ref.shape[2]
-    pieces = sems.shape[0]
+    pieces = sems.shape[0] - 1
+    layer = pltpu.make_async_copy(layer_ref, layer_out_ref, sems.at[pieces])
+    layer.start()
     rows = held.shape[0] // pieces
     copies = []
     for i in range(pieces):
@@ -62,6 +65,7 @@
         copies.append(copy)
     for copy in copies:
         copy.wait()
+    layer.wait()
 
 
 def layer_kernel(
@@ -75,7 +79,7 @@
     table_ref,
     w_in_ref,
     w_out_ref,
-    og_ref,
+    og_in_ref,
     out_ref,
     grads_ref,
     xg,
@@ -112,6 +116,7 @@
     w_in,
     w_out,
     looked,
+    og_ref,
     local_sems,
 ):
     me = lax.axis_index("ctx")
@@ -125,7 +130,7 @@
     hd = width // H
     scale = hd ** (-0.5)
 
-    pieces = local_sems.shape[0] - 2
+    pieces = local_sems.shape[0] - 3
     piece = held.shape[0] // pieces
     loads = [
         pltpu.make_async_copy(
@@ -140,6 +145,8 @@
     for load in loads:
         load.start()
     load_out.start()
+    load_og = pltpu.make_async_copy(og_in_ref, og_ref, local_sems.at[pieces + 2])
+    load_og.start()
     load_in.start()
 
     barrier = pltpu.get_barrier_semaphore()
@@ -221,6 +228,7 @@
         route_copy(route_out, route_in, rs, rr, lax.rem(tab + k, tabs)).start()
 
     load_out.wait()
+    load_og.wait()
     dm[...] = dot_nt(og_ref[0], w_out[...])
 
     def starts_of(pos):
@@ -363,9 +371,27 @@
             def _():
                 action(copy(s, side, 1))
 
-            @pl.when(needed(partner, s, side))
+            if side == ALONG:
+                beside = (zz == z - 1) | (zz == z + 1)
+                has = needed(zz * FAST + (FAST - 1 - x), s, side)
+                across = needed(partner, s, side) & ~(beside & has)
+            else:
+                across = needed(partner, s, side)
+
+            @pl.when(across)
             def _():
                 action(copy(s, side, 2))
+
+        def along(action):
+            has = needed(me, partner, ALONG)
+
+            @pl.when(has & (z > 0) & needed(me - FAST, partner, ALONG))
+            def _():
+                action(copy(partner, ALONG, 0))
+
+            @pl.when(has & (z < levels - 1) & needed(me + FAST, partner, ALONG))
+            def _():
+                action(copy(partner, ALONG, 1))
 
         def level(k, i):
             zz = z + jnp.where(i == 0, -k, k)
@@ -388,6 +414,10 @@
 
                         ways(zz, side, lambda c: c.start())
 
+            @pl.when(k == 2)
+            def _():
+                along(lambda c: c.start())
+
             filler(k)
 
             def own_column(i, carry):
@@ -400,9 +430,10 @@
                 return carry
 
             def other_column(i, carry):
-                zz, there = level(k - 1, i)
-
-                @pl.when(there)
+                last = k == levels + 1
+                zz, there = level(jnp.where(last, 1, k - 1), i)
+
+                @pl.when(there & ((k != 2) | last))
                 def _():
                     s = zz * FAST + (FAST - 1 - x)
                     for side in range(2):
@@ -419,7 +450,7 @@
             lax.fori_loop(0, 2, other_column, 0)
             return carry
 
-        lax.fori_loop(0, levels + 1, step, 0)
+        lax.fori_loop(0, levels + 2, step, 0)
 
         def drain(zz, carry):
             for side in range(2):
@@ -427,6 +458,7 @@
             return carry
 
         lax.fori_loop(0, levels, drain, 0)
+        along(lambda c: c.wait_send())
 
     load_in.wait()
     for k in range(1, tabs):
@@ -559,7 +591,7 @@
             jax.ShapeDtypeStruct((1, count, width), bf16),
             jax.ShapeDtypeStruct((count, width), bf16),
         ),
-        in_specs=[smem] * 4 + [vmem, hbm, hbm, hbm, vmem],
+        in_specs=[smem] * 4 + [vmem, hbm, hbm, hbm, hbm],
         out_specs=(vmem, vmem),
         scratch_shapes=[
             pltpu.VMEM((n, count, width), bf16),
@@ -596,21 +628,25 @@
             pltpu.VMEM(w_in.shape, bf16),
             pltpu.VMEM(w_out.shape, bf16),
             pltpu.VMEM((count, width), bf16),
-            dma((pieces + 2,)),
+            pltpu.VMEM(og.shape, bf16),
+            dma((pieces + 3,)),
         ],
         compiler_params=pltpu.CompilerParams(
             collective_id=0, has_side_effects=True, vmem_limit_bytes=60 * 1024 * 1024
         ),
         name="layer",
     )(dests, slots, lengths, tile_mask, row_ids, table, w_in, w_out, og)
-    table_grad = pl.pallas_call(
+    table_grad, layer_out = pl.pallas_call(
         scatter_kernel,
-        out_shape=jax.ShapeDtypeStruct((1, 1, table_rows, width), bf16),
-        in_specs=[vmem, vmem],
-        out_specs=hbm,
-        scratch_shapes=[pltpu.VMEM((table_rows, width), bf16), dma((pieces,))],
+        out_shape=(
+            jax.ShapeDtypeStruct((1, 1, table_rows, width), bf16),
+            jax.ShapeDtypeStruct((1, count, width), bf16),
+        ),
+        in_specs=[vmem, vmem, vmem],
+        out_specs=(hbm, hbm),
+        scratch_shapes=[pltpu.VMEM((table_rows, width), bf16), dma((pieces + 1,))],
         name="table_grad",
-    )(row_ids, row_grads)
+    )(row_ids, row_grads, layer_out)
     return layer_out, table_grad
 
 

time: 71.7 us -> 72.4 us (level); the launches traced: 71.6 us -> 71.2 us
  no operation moved by 1% of the time
where the time goes in v4:
time: 72.4 us; the launch traced here: 71.2 us
  Pallas kernels  70.5 us (97%)
    pallas_call x1, Pallas kernels, body(): pl.pallas_call(functools.partial(layer_kernel, n, tabs), out_shape=(jax.S...  67.1 us
    pallas_call x1, Pallas kernels, body(): pl.pallas_call(scatter_kernel, out_shape=(jax.ShapeDtypeStruct((1, 1, tab...  3.43 us

profile of v4, /device:TPU:1, one launch (start us, length us, event | category | flops | bytes accessed | tf_op | source)
XLA Modules:
  0.0 71.2 jit_solution(1413899372958680627)
XLA Ops:
  0.6 67.1 %layer.1 = (bf16[1,256,512]{2,1,0:T(8,128)(2,1)}, bf16[256,512]{1,0:T(8,128)(2,1)}) custom-call(s32[1,4,4]{2,1,0:T(4,128)} %dests.1, s32[1,4,4]{2,1,0:T(4,128)} %slots.1, s32[1,16]{1,0:T(1,128)} %lengths.1, s32[1,32,32]{2,1,0:T(8,128)} %tiles.1, s32[1,1,256]{2,1,0:T(1,128)} %ids_ref.3, bf16[1,1,4096,512]{3,2,1,0:T(8,128)(2,1)} %table_ref.1, ...), custom_call_target="tpu_custom_call" | custom-call | tf_op jit(solution)/shard_map/layer/pallas_call | solution.py:588
  67.7 3.4 %table_grad.1 = (bf16[1,1,4096,512]{3,2,1,0:T(8,128)(2,1)}, bf16[1,256,512]{2,1,0:T(8,128)(2,1)}) custom-call(s32[1,1,256]{2,1,0:T(1,128)} %ids_ref.3, bf16[256,512]{1,0:T(8,128)(2,1)} %get-tuple-element.6.grads_ref, bf16[1,256,512]{2,1,0:T(8,128)(2,1)} %get-tuple-element.7.layer_ref), custom_call_target="tpu_custom_call" | custom-call | tf_op jit(solution)/shard_map/table_grad/pallas_call | solution.py:639

commit v5 on v4

--- a/solution.py
+++ b/solution.py
@@ -11,7 +11,6 @@
 BROWS = 64
 NBLK = 4
 FAST = 2
-ALONG = 1
 
 epsilon = 1e-05
 MESH = pl.DeviceIdType.MESH
@@ -100,6 +99,7 @@
     xhat,
     xinv,
     startq,
+    startk,
     route_out,
     route_in,
     back_out,
@@ -245,15 +245,19 @@
     for side in range(2):
         local = lax.broadcasted_iota(jnp.int32, (half, 128), 0)
         startq[side * half : (side + 1) * half, :] = starts_of(local + base_of(me, side))
+    chunk = lax.broadcasted_iota(jnp.int32, (2 * n, half), 0)
+    startk[...] = starts_of(
+        chunk * half + lax.broadcasted_iota(jnp.int32, (2 * n, half), 1)
+    )
     attn[...] = jnp.zeros_like(attn)
 
     def tile_rows(pick):
-        block = lax.broadcasted_iota(jnp.int32, (BROWS, half), 1) // BROWS
+        lane = lax.broadcasted_iota(jnp.int32, (BROWS, half), 1)
         stripes = []
         for a in range(per_half):
             line = jnp.full((BROWS, half), pick(a, 0))
             for b in range(1, per_half):
-                line = jnp.where(block == b, pick(a, b), line)
+                line = jnp.where(lane >= b * BROWS, pick(a, b), line)
             stripes.append(line)
         return jnp.concatenate(stripes, axis=0) > 0
 
@@ -270,7 +274,7 @@
         at, to = base_of(me, mine), base_of(s, theirs)
         own = lax.broadcasted_iota(jnp.int32, (half, half), 0) + at
         other = lax.broadcasted_iota(jnp.int32, (half, half), 1) + to
-        first = starts_of(lax.broadcasted_iota(jnp.int32, (1, half), 1) + to)
+        first = startk[pl.ds(to // half, 1), :]
         at, to = at // BROWS, to // BROWS
         on = tile_rows(lambda a, b: tiles[0, to + b, at + a])
         return jnp.where((own <= other) & (own >= first) & on, 1.0, 0.0)
@@ -295,27 +299,46 @@
             (s >= me, 1, 1, 0, 0),
         )
 
-    def forward(s):
+    def scores(q, k, mask, halved):
+        halfs = dot_nt(q, k) * (0.5 * scale)
+        grown = 1.0 + jnp.tanh(halfs)
+        value = halfs * grown
+        slope = grown + value * (2.0 - grown)
+        return (value * mask).astype(jnp.bfloat16), (slope * halved).astype(jnp.bfloat16)
+
+    def key_forward(s):
+        for i, (when, _, _, km, qt) in enumerate(quads(s)):
+
+            @pl.when(when)
+            def _(i=i, km=km, qt=qt):
+                mask = key_mask(s, km, qt)
+                halved = mask * (0.5 * scale)
+                for h in range(H):
+                    pk[i, s, h], gk[i, s, h] = scores(
+                        take(2, me, km, h), take(1, s, qt, h), mask, halved
+                    )
+
+    def forward(s, both):
         project(s)
         for i, (when, qm, kt, km, qt) in enumerate(quads(s)):
 
             @pl.when(when)
             def _(i=i, qm=qm, kt=kt, km=km, qt=qt):
                 mask = query_mask(s, qm, kt)
-                scaled = mask * scale
-                mask_k = key_mask(s, km, qt)
-                scaled_k = mask_k * scale
+                halved = mask * (0.5 * scale)
+                if both:
+                    mask_k = key_mask(s, km, qt)
+                    halved_k = mask_k * (0.5 * scale)
                 for h in range(H):
                     cut = slice(h * hd, (h + 1) * hd)
-                    halfs = dot_nt(take(1, me, qm, h), take(2, s, kt, h)) * (0.5 * scale)
-                    tanh = jnp.tanh(halfs)
-                    probs = (halfs * (1.0 + tanh) * mask).astype(jnp.bfloat16)
-                    gq[i, s, h] = (slope_half(halfs, tanh) * scaled).astype(jnp.bfloat16)
+                    probs, gq[i, s, h] = scores(
+                        take(1, me, qm, h), take(2, s, kt, h), mask, halved
+                    )
                     attn[side_rows(qm), cut] += dot(probs, take(0, s, kt, h))
-                    halfs = dot_nt(take(2, me, km, h), take(1, s, qt, h)) * (0.5 * scale)
-                    tanh = jnp.tanh(halfs)
-                    pk[i, s, h] = (halfs * (1.0 + tanh) * mask_k).astype(jnp.bfloat16)
-                    gk[i, s, h] = (slope_half(halfs, tanh) * scaled_k).astype(jnp.bfloat16)
+                    if both:
+                        pk[i, s, h], gk[i, s, h] = scores(
+                            take(2, me, km, h), take(1, s, qt, h), mask_k, halved_k
+                        )
 
     def query_back(s):
         for i, (when, qm, kt, _, _) in enumerate(quads(s)):
@@ -330,7 +353,7 @@
                         dsc.astype(jnp.bfloat16), take(2, s, kt, h)
                     )
 
-    def key_back(s):
+    def key_back(s, _):
         for i, (when, _, _, km, qt) in enumerate(quads(s)):
 
             @pl.when(when)
@@ -345,6 +368,11 @@
                     )
                     dv[side_rows(km), cut] += dot(pk[i, s, h], grad)
 
+    def level(k, i):
+        zz = z + jnp.where(i == 0, -k, k)
+        there = (k >= 0) & (k < levels) & (zz >= 0) & (zz < levels)
+        return zz, there & ((k > 0) | (i == 0))
+
     def gather(buf, send, recv, wanted, needed, compute, filler):
         partner = z * FAST + (FAST - 1 - x)
 
@@ -371,32 +399,9 @@
             def _():
                 action(copy(s, side, 1))
 
-            if side == ALONG:
-                beside = (zz == z - 1) | (zz == z + 1)
-                has = needed(zz * FAST + (FAST - 1 - x), s, side)
-                across = needed(partner, s, side) & ~(beside & has)
-            else:
-                across = needed(partner, s, side)
-
-            @pl.when(across)
+            @pl.when(needed(partner, s, side))
             def _():
                 action(copy(s, side, 2))
-
-        def along(action):
-            has = needed(me, partner, ALONG)
-
-            @pl.when(has & (z > 0) & needed(me - FAST, partner, ALONG))
-            def _():
-                action(copy(partner, ALONG, 0))
-
-            @pl.when(has & (z < levels - 1) & needed(me + FAST, partner, ALONG))
-            def _():
-                action(copy(partner, ALONG, 1))
-
-        def level(k, i):
-            zz = z + jnp.where(i == 0, -k, k)
-            there = (k >= 0) & (k < levels) & (zz >= 0) & (zz < levels)
-            return zz, there & ((k > 0) | (i == 0))
 
         def step(k, carry):
             for i in range(2):
@@ -414,10 +419,6 @@
 
                         ways(zz, side, lambda c: c.start())
 
-            @pl.when(k == 2)
-            def _():
-                along(lambda c: c.start())
-
             filler(k)
 
             def own_column(i, carry):
@@ -425,15 +426,14 @@
 
                 @pl.when(there)
                 def _():
-                    compute(zz * FAST + x)
+                    compute(zz * FAST + x, True)
 
                 return carry
 
             def other_column(i, carry):
-                last = k == levels + 1
-                zz, there = level(jnp.where(last, 1, k - 1), i)
-
-                @pl.when(there & ((k != 2) | last))
+                zz, there = level(k - 1, i)
+
+                @pl.when(there)
                 def _():
                     s = zz * FAST + (FAST - 1 - x)
                     for side in range(2):
@@ -442,7 +442,7 @@
                         def _(side=side):
                             copy(s, side, 2).wait_recv()
 
-                    compute(s)
+                    compute(s, False)
 
                 return carry
 
@@ -450,7 +450,7 @@
             lax.fori_loop(0, 2, other_column, 0)
             return carry
 
-        lax.fori_loop(0, levels + 2, step, 0)
+        lax.fori_loop(0, levels + 1, step, 0)
 
         def drain(zz, carry):
             for side in range(2):
@@ -458,7 +458,6 @@
             return carry
 
         lax.fori_loop(0, levels, drain, 0)
-        along(lambda c: c.wait_send())
 
     load_in.wait()
     for k in range(1, tabs):
@@ -530,6 +529,17 @@
                 return carry
 
             lax.fori_loop(0, FAST, one, 0)
+
+        def two(i, carry):
+            zz, there = level(j - 1, i)
+
+            @pl.when(there)
+            def _():
+                key_forward(zz * FAST + (FAST - 1 - x))
+
+            return carry
+
+        lax.fori_loop(0, 2, two, 0)
 
         @pl.when(j == levels)
         def _():
@@ -612,6 +622,7 @@
             pltpu.VMEM((count, width), f32),
             pltpu.VMEM((count, 128), f32),
             pltpu.VMEM((count, 128), jnp.int32),
+            pltpu.VMEM((2 * n, count // 2), jnp.int32),
             pltpu.VMEM((tabs, BROWS, width), bf16),
             pltpu.VMEM((tabs, BROWS, width), bf16),
             pltpu.VMEM((tabs, BROWS, width), bf16),

time: 72.4 us -> 72 us (level); the launches traced: 71.2 us -> 71.8 us
  no operation moved by 1% of the time
where the time goes in v5:
time: 72 us; the launch traced here: 71.8 us
  Pallas kernels  71.1 us (99%)
    pallas_call x1, Pallas kernels, body(): pl.pallas_call(functools.partial(layer_kernel, n, tabs), out_shape=(jax.S...  67.7 us
    pallas_call x1, Pallas kernels, body(): pl.pallas_call(scatter_kernel, out_shape=(jax.ShapeDtypeStruct((1, 1, tab...  3.43 us

profile of v5, /device:TPU:1, one launch (start us, length us, event | category | flops | bytes accessed | tf_op | source)
XLA Modules:
  0.0 71.8 jit_solution(16503475054511474769)
XLA Ops:
  0.6 67.7 %layer.1 = (bf16[1,256,512]{2,1,0:T(8,128)(2,1)}, bf16[256,512]{1,0:T(8,128)(2,1)}) custom-call(s32[1,4,4]{2,1,0:T(4,128)} %dests.1, s32[1,4,4]{2,1,0:T(4,128)} %slots.1, s32[1,16]{1,0:T(1,128)} %lengths.1, s32[1,32,32]{2,1,0:T(8,128)} %tiles.1, s32[1,1,256]{2,1,0:T(1,128)} %ids_ref.3, bf16[1,1,4096,512]{3,2,1,0:T(8,128)(2,1)} %table_ref.1, ...), custom_call_target="tpu_custom_call" | custom-call | tf_op jit(solution)/shard_map/layer/pallas_call | solution.py:598
  68.3 3.4 %table_grad.1 = (bf16[1,1,4096,512]{3,2,1,0:T(8,128)(2,1)}, bf16[1,256,512]{2,1,0:T(8,128)(2,1)}) custom-call(s32[1,1,256]{2,1,0:T(1,128)} %ids_ref.3, bf16[256,512]{1,0:T(8,128)(2,1)} %get-tuple-element.6.grads_ref, bf16[1,256,512]{2,1,0:T(8,128)(2,1)} %get-tuple-element.7.layer_ref), custom_call_target="tpu_custom_call" | custom-call | tf_op jit(solution)/shard_map/table_grad/pallas_call | solution.py:650
